TPU v7x, 32 devices: a whole 2x2x4 slice. The times are simulated.
32 devices in a mesh: seq: 8 (over z, core), fsdp: 4 (over y, x).
Axes of the slice: x: 2, y: 2, z: 4, core: 2. Of those that a mesh axis runs over, the one named last changes fastest.
Arguments:
- tokens: bfloat16 [4, 1024, 2048], P('fsdp', 'seq'), may hold values from -6 to 6
- segments: int32 [4, 1024], P('fsdp'), may hold values from 0 to 5, never falling along the last dimension, each value on 1 to 512 neighbouring positions
- cotangent: bfloat16 [4, 1024, 2048], P('fsdp', 'seq'), may hold values from -6 to 6
- mix_weight: float32 [2048, 6144], P(('seq', 'fsdp')), may hold values from -0.125 to 0.125
- mix_moment: float32 [2048, 6144], P(('seq', 'fsdp')), may hold values from -112 to 112
- mix_average: float32 [2048, 6144], P(('seq', 'fsdp')), may hold values from -0.125 to 0.125
- out_weight: float32 [2048, 2048], P(('seq', 'fsdp')), may hold values from -0.375 to 0.375
- out_moment: float32 [2048, 2048], P(('seq', 'fsdp')), may hold values from -112 to 112
- out_average: float32 [2048, 2048], P(('seq', 'fsdp')), may hold values from -0.375 to 0.375
- up_weight: float32 [2048, 8192], P(('seq', 'fsdp')), may hold values from -0.125 to 0.125
- up_moment: float32 [2048, 8192], P(('seq', 'fsdp')), may hold values from -112 to 112
- up_average: float32 [2048, 8192], P(('seq', 'fsdp')), may hold values from -0.125 to 0.125
- down_weight: float32 [8192, 2048], P(('seq', 'fsdp')), may hold values from -0.0625 to 0.0625
- down_moment: float32 [8192, 2048], P(('seq', 'fsdp')), may hold values from -112 to 112
- down_average: float32 [8192, 2048], P(('seq', 'fsdp')), may hold values from -0.0625 to 0.0625
- norm_gains: float32 [2, 2048], P(None, ('seq', 'fsdp')), may hold values from 0.1 to 1.9
- gain_moment: float32 [2, 2048], P(None, ('seq', 'fsdp')), may hold values from -192 to 192
- gain_average: float32 [2, 2048], P(None, ('seq', 'fsdp')), may hold values from 0.1 to 1.9
- biases: float32 [10, 2048], P(None, ('seq', 'fsdp')), may hold values from -3 to 3
- bias_moment: float32 [10, 2048], P(None, ('seq', 'fsdp')), may hold values from -192 to 192
- bias_average: float32 [10, 2048], P(None, ('seq', 'fsdp')), may hold values from -3 to 3
Outputs:
- output: bfloat16 [4, 1024, 2048], P('fsdp', 'seq')
- tokens_grad: bfloat16 [4, 1024, 2048], P('fsdp', 'seq')
- mix_moment_new: float32 [2048, 6144], P(('seq', 'fsdp'))
- mix_weight_new: float32 [2048, 6144], P(('seq', 'fsdp'))
- mix_average_new: float32 [2048, 6144], P(('seq', 'fsdp'))
- out_moment_new: float32 [2048, 2048], P(('seq', 'fsdp'))
- out_weight_new: float32 [2048, 2048], P(('seq', 'fsdp'))
- out_average_new: float32 [2048, 2048], P(('seq', 'fsdp'))
- up_moment_new: float32 [2048, 8192], P(('seq', 'fsdp'))
- up_weight_new: float32 [2048, 8192], P(('seq', 'fsdp'))
- up_average_new: float32 [2048, 8192], P(('seq', 'fsdp'))
- down_moment_new: float32 [8192, 2048], P(('seq', 'fsdp'))
- down_weight_new: float32 [8192, 2048], P(('seq', 'fsdp'))
- down_average_new: float32 [8192, 2048], P(('seq', 'fsdp'))
- gain_moment_new: float32 [2, 2048], P(None, ('seq', 'fsdp'))
- gain_weight_new: float32 [2, 2048], P(None, ('seq', 'fsdp'))
- gain_average_new: float32 [2, 2048], P(None, ('seq', 'fsdp'))
- bias_moment_new: float32 [10, 2048], P(None, ('seq', 'fsdp'))
- bias_weight_new: float32 [10, 2048], P(None, ('seq', 'fsdp'))
- bias_average_new: float32 [10, 2048], P(None, ('seq', 'fsdp'))
Inputs may be any that keep to these rules, and one draw needn't show every extreme that they name: `segments`: document numbers never fall along a sequence; each document holds 1 to 512 tokens, one exactly that many.
All inputs are finite; a program needn't handle non-finite values.
Results may differ from a plain program's by a relative error of at most 0.02.
Values may be sent and summed in bfloat16 or wider, within the bound.
A program may use at most 512 MiB of HBM per device.

v0:
```python
import math

import jax
import jax.numpy as jnp
from jax import lax
from jax.sharding import PartitionSpec as P

D = 2048
HEADS = 32
HD = 64
FF = 8192


epsilon = 1e-05
mom_decay = 0.5
avg_decay = 0.5
base_rate = 0.02
vector_rate = 0.1


def layer_norm(values, gain_row, shift_row):
    centred = values - jnp.mean(values, axis=-1, keepdims=True)
    spread = jnp.mean(centred * centred, axis=-1, keepdims=True)
    return centred * lax.rsqrt(spread + epsilon) * gain_row + shift_row


def gelu_exact(values):
    return jax.nn.gelu(values, approximate=False)


def block_logits(query_block, key_block, query_start, key_start, documents, slopes):
    block_size = query_block.shape[0]
    raw_scores = jnp.einsum(
        "qhd,khd->hqk", query_block, key_block, preferred_element_type=jnp.float32
    )
    query_position = query_start + jnp.arange(block_size, dtype=jnp.int32)
    key_position = key_start + jnp.arange(block_size, dtype=jnp.int32)
    query_docs = lax.dynamic_slice_in_dim(documents, query_start, block_size)
    key_docs = lax.dynamic_slice_in_dim(documents, key_start, block_size)
    distance = (query_position[:, None] - key_position[None, :]).astype(jnp.float32)
    logits = raw_scores * HD ** (-0.5) - slopes[:, None, None] * distance
    allowed = (key_position[None, :] <= query_position[:, None]) & (
        query_docs[:, None] == key_docs[None, :]
    )
    return jnp.where(allowed[None], logits, -1000000000.0)


def attend_forward(queries, key_heads, values, documents, slopes, block_rows):
    seq_length, head_count, head_size = queries.shape
    block_count = seq_length // block_rows

    def one_block(query_index):
        query_start = query_index * block_rows
        query_block = lax.dynamic_slice_in_dim(queries, query_start, block_rows)

        def statistics(key_index, carried):
            run_max, run_sum = carried
            key_start = key_index * block_rows
            logits = block_logits(
                query_block,
                lax.dynamic_slice_in_dim(key_heads, key_start, block_rows),
                query_start,
                key_start,
                documents,
                slopes,
            )
            new_max = jnp.maximum(run_max, jnp.max(logits, axis=-1))
            run_sum = run_sum * jnp.exp(run_max - new_max) + jnp.sum(
                jnp.exp(logits - new_max[..., None]), axis=-1
            )
            return (new_max, run_sum)

        initial = (
            jnp.full((head_count, block_rows), -1e30, jnp.float32),
            jnp.zeros((head_count, block_rows), jnp.float32),
        )
        run_max, run_sum = lax.fori_loop(0, query_index + 1, statistics, initial)
        log_sum = run_max + jnp.log(run_sum)

        def collect(key_index, summed):
            key_start = key_index * block_rows
            logits = block_logits(
                query_block,
                lax.dynamic_slice_in_dim(key_heads, key_start, block_rows),
                query_start,
                key_start,
                documents,
                slopes,
            )
            weights = jnp.exp(logits - log_sum[..., None]).astype(jnp.bfloat16)
            value_block = lax.dynamic_slice_in_dim(values, key_start, block_rows)
            return summed + jnp.einsum(
                "hqk,khd->qhd", weights, value_block, preferred_element_type=jnp.float32
            )

        summed = lax.fori_loop(
            0, query_index + 1, collect, jnp.zeros((block_rows, head_count, head_size), jnp.float32)
        )
        return (summed.astype(jnp.bfloat16), log_sum)

    blocks, log_sums = lax.map(one_block, jnp.arange(block_count, dtype=jnp.int32))
    return (blocks.reshape(seq_length, head_count, head_size), log_sums)


def attend_backward(
    queries, key_heads, values, attended, upstream, log_sums, documents, slopes, block_rows
):
    seq_length, head_count, head_size = queries.shape
    block_count = seq_length // block_rows
    score_scale = HD ** (-0.5)
    deltas = jnp.sum(attended.astype(jnp.float32) * upstream.astype(jnp.float32), axis=-1).T

    def key_step(query_grads, key_index):
        key_start = key_index * block_rows
        key_block = lax.dynamic_slice_in_dim(key_heads, key_start, block_rows)
        value_block = lax.dynamic_slice_in_dim(values, key_start, block_rows)

        def query_step(query_index, carried):
            key_grad, value_grad, query_all = carried
            query_start = query_index * block_rows
            query_block = lax.dynamic_slice_in_dim(queries, query_start, block_rows)
            upstream_block = lax.dynamic_slice_in_dim(upstream, query_start, block_rows)
            logits = block_logits(query_block, key_block, query_start, key_start, documents, slopes)
            log_row = lax.dynamic_index_in_dim(log_sums, query_index, 0, keepdims=False)
            prob_block = jnp.exp(logits - log_row[..., None])
            prob_grads = jnp.einsum(
                "qhd,khd->hqk", upstream_block, value_block, preferred_element_type=jnp.float32
            )
            delta_block = lax.dynamic_slice_in_dim(deltas, query_start, block_rows, axis=1)
            logit_grads = (prob_block * (prob_grads - delta_block[..., None])).astype(jnp.bfloat16)
            value_grad = value_grad + jnp.einsum(
                "hqk,qhd->khd",
                prob_block.astype(jnp.bfloat16),
                upstream_block,
                preferred_element_type=jnp.float32,
            )
            key_grad = key_grad + jnp.einsum(
                "hqk,qhd->khd", logit_grads, query_block, preferred_element_type=jnp.float32
            )
            update = jnp.einsum(
                "hqk,khd->qhd", logit_grads, key_block, preferred_element_type=jnp.float32
            )
            current = lax.dynamic_slice_in_dim(query_all, query_start, block_rows)
            query_all = lax.dynamic_update_slice_in_dim(query_all, current + update, query_start, 0)
            return (key_grad, value_grad, query_all)

        zero_block = jnp.zeros((block_rows, head_count, head_size), jnp.float32)
        key_grad, value_grad, query_grads = lax.fori_loop(
            key_index, block_count, query_step, (zero_block, zero_block, query_grads)
        )
        return (query_grads, (key_grad * score_scale, value_grad))

    query_grads, (key_grads, value_grads) = lax.scan(
        key_step,
        jnp.zeros((seq_length, head_count, head_size), jnp.float32),
        jnp.arange(block_count, dtype=jnp.int32),
    )
    shape = (seq_length, head_count, head_size)
    return (query_grads * score_scale, key_grads.reshape(shape), value_grads.reshape(shape))


def body(
    tokens,
    segments,
    cotangent,
    mix_weight,
    mix_moment,
    mix_average,
    out_weight,
    out_moment,
    out_average,
    up_weight,
    up_moment,
    up_average,
    down_weight,
    down_moment,
    down_average,
    norm_gains,
    gain_moment,
    gain_average,
    biases,
    bias_moment,
    bias_average,
):
    groups = lax.axis_size("seq")
    owners = groups * lax.axis_size("fsdp")
    seq_index = lax.axis_index("seq")
    tok_count = tokens.shape[1]
    seq_length = tok_count * groups
    local_heads = HEADS // groups
    width_local = local_heads * HD
    block_rows = min(512, seq_length)
    head_ids = seq_index * local_heads + jnp.arange(local_heads, dtype=jnp.int32) + 1
    slopes = jnp.exp2(-8.0 * head_ids.astype(jnp.float32) / HEADS)
    documents = segments[0]
    masters = (mix_weight, out_weight, up_weight, down_weight, norm_gains, biases)
    lowered = tuple((master.astype(jnp.bfloat16) for master in masters))
    gathered = (
        lax.all_gather(lowered[0], ("seq", "fsdp"), axis=0, tiled=True),
        lax.all_gather(lowered[1], ("seq", "fsdp"), axis=0, tiled=True),
        lax.all_gather(lowered[2], ("seq", "fsdp"), axis=0, tiled=True),
        lax.all_gather(lowered[3], ("seq", "fsdp"), axis=0, tiled=True),
        lax.all_gather(lowered[4], ("seq", "fsdp"), axis=1, tiled=True),
        lax.all_gather(lowered[5], ("seq", "fsdp"), axis=1, tiled=True),
    )
    mix_full, out_full, up_full, down_full, gains_full, biases_full = gathered
    gain_values = gains_full.astype(jnp.float32)
    bias_values = biases_full.astype(jnp.float32)
    row_values = tokens[0].astype(jnp.float32)
    normed = layer_norm(row_values, gain_values[0], bias_values[0]).astype(jnp.bfloat16)
    mix_bias = jnp.concatenate([bias_values[1], jnp.zeros((D,), jnp.float32), bias_values[2]])
    mixed_rows = (jnp.dot(normed, mix_full, preferred_element_type=jnp.float32) + mix_bias).astype(
        jnp.bfloat16
    )
    by_heads = lax.all_to_all(
        mixed_rows.reshape(tok_count, 3, groups, width_local),
        "seq",
        split_axis=2,
        concat_axis=0,
        tiled=True,
    )
    queries = by_heads[:, 0, 0].reshape(seq_length, local_heads, HD)
    key_heads = by_heads[:, 1, 0].reshape(seq_length, local_heads, HD)
    values = by_heads[:, 2, 0].reshape(seq_length, local_heads, HD)
    attended, log_sums = attend_forward(queries, key_heads, values, documents, slopes, block_rows)
    back_rows = lax.all_to_all(
        attended.reshape(seq_length, 1, width_local), "seq", split_axis=0, concat_axis=1, tiled=True
    )
    attn_rows = back_rows.reshape(tok_count, D)
    hidden_in = (
        row_values
        + jnp.dot(attn_rows, out_full, preferred_element_type=jnp.float32)
        + bias_values[3]
    )
    normed_two = layer_norm(hidden_in, gain_values[1], bias_values[4]).astype(jnp.bfloat16)
    pre_act = jnp.dot(normed_two, up_full, preferred_element_type=jnp.float32) + bias_values[
        6:10
    ].reshape(FF)
    activated = gelu_exact(pre_act).astype(jnp.bfloat16)
    result = (
        hidden_in
        + jnp.dot(activated, down_full, preferred_element_type=jnp.float32)
        + bias_values[5]
    )
    output = result.astype(jnp.bfloat16)[None]
    regathered = (
        lax.all_gather(lowered[0], ("seq", "fsdp"), axis=0, tiled=True),
        lax.all_gather(lowered[1], ("seq", "fsdp"), axis=0, tiled=True),
        lax.all_gather(lowered[2], ("seq", "fsdp"), axis=0, tiled=True),
        lax.all_gather(lowered[3], ("seq", "fsdp"), axis=0, tiled=True),
    )
    mix_back, out_back, up_back, down_back = regathered
    upstream_rows = cotangent[0]
    upstream_float = upstream_rows.astype(jnp.float32)
    down_share = lax.psum_scatter(
        jnp.einsum("tf,td->fd", activated, upstream_rows, preferred_element_type=jnp.float32),
        ("seq", "fsdp"),
        scatter_dimension=0,
        tiled=True,
    )
    activated_gradient = jnp.einsum(
        "td,fd->tf", upstream_rows, down_back, preferred_element_type=jnp.float32
    )
    pre_gradient = jax.vjp(gelu_exact, pre_act)[1](activated_gradient)[0].astype(jnp.bfloat16)
    normed_two_gradient = jnp.einsum(
        "tf,cf->tc", pre_gradient, up_back, preferred_element_type=jnp.float32
    )
    second_pull = jax.vjp(layer_norm, hidden_in, gain_values[1], bias_values[4])[1]
    hidden_part, gain_two_gradient, shift_two_gradient = second_pull(normed_two_gradient)
    hidden_gradient = upstream_float + hidden_part
    hidden_low = hidden_gradient.astype(jnp.bfloat16)
    attn_gradient = jnp.einsum(
        "td,cd->tc", hidden_low, out_back, preferred_element_type=jnp.float32
    ).astype(jnp.bfloat16)
    upstream_heads = lax.all_to_all(
        attn_gradient.reshape(tok_count, groups, width_local),
        "seq",
        split_axis=1,
        concat_axis=0,
        tiled=True,
    )
    upstream_heads = upstream_heads.reshape(seq_length, local_heads, HD)
    query_grads, key_grads, value_grads = attend_backward(
        queries,
        key_heads,
        values,
        attended,
        upstream_heads,
        log_sums,
        documents,
        slopes,
        block_rows,
    )
    stacked = (
        jnp.stack([query_grads, key_grads, value_grads], axis=1)
        .astype(jnp.bfloat16)
        .reshape(seq_length, 3, 1, width_local)
    )
    returned = lax.all_to_all(stacked, "seq", split_axis=0, concat_axis=2, tiled=True).reshape(
        tok_count, 3 * D
    )
    normed_gradient = jnp.einsum(
        "te,ce->tc", returned, mix_back, preferred_element_type=jnp.float32
    )
    first_pull = jax.vjp(layer_norm, row_values, gain_values[0], bias_values[0])[1]
    rows_part, gain_one_gradient, shift_one_gradient = first_pull(normed_gradient)
    tokens_grad = (hidden_gradient + rows_part).astype(jnp.bfloat16)[None]
    returned_float = returned.astype(jnp.float32)
    gains_gradient = jnp.stack([gain_one_gradient, gain_two_gradient])
    first_rows = jnp.stack(
        [
            shift_one_gradient,
            jnp.sum(returned_float[:, :D], axis=0),
            jnp.sum(returned_float[:, 2 * D :], axis=0),
            jnp.sum(hidden_gradient, axis=0),
            shift_two_gradient,
            jnp.sum(upstream_float, axis=0),
        ]
    )
    up_bias_rows = jnp.sum(pre_gradient.astype(jnp.float32), axis=0).reshape(4, D)
    small_gradient = jnp.concatenate([gains_gradient, first_rows, up_bias_rows], axis=0)
    small_part = small_gradient.T
    mix_part = jnp.einsum("tc,te->ce", normed, returned, preferred_element_type=jnp.float32)
    out_part = jnp.einsum("tc,td->cd", attn_rows, hidden_low, preferred_element_type=jnp.float32)
    up_part = jnp.einsum("tc,tf->cf", normed_two, pre_gradient, preferred_element_type=jnp.float32)
    width_share = lax.psum_scatter(
        jnp.concatenate([mix_part, out_part, up_part, small_part], axis=1),
        ("seq", "fsdp"),
        scatter_dimension=0,
        tiled=True,
    )
    mix_share = width_share[:, : 3 * D]
    out_share = width_share[:, 3 * D : 4 * D]
    up_share = width_share[:, 4 * D : 4 * D + FF]
    gain_share = width_share[:, 4 * D + FF : 4 * D + FF + 2].T
    bias_share = width_share[:, 4 * D + FF + 2 : 4 * D + FF + 12].T
    step_rate = base_rate / math.sqrt(owners * tok_count)
    vector_step = vector_rate / math.sqrt(owners * tok_count)
    rate_list = (step_rate, step_rate, step_rate, step_rate, vector_step, vector_step)
    shares = (mix_share, out_share, up_share, down_share, gain_share, bias_share)
    moments = (mix_moment, out_moment, up_moment, down_moment, gain_moment, bias_moment)
    averages = (mix_average, out_average, up_average, down_average, gain_average, bias_average)
    updated = []
    for master, moment, average, share, rate in zip(masters, moments, averages, shares, rate_list):
        new_moment = mom_decay * moment + share
        new_weight = master - rate * (share + mom_decay * new_moment)
        new_average = avg_decay * average + (1.0 - avg_decay) * new_weight
        updated += [new_moment, new_weight, new_average]
    return (
        output,
        tokens_grad,
        updated[0],
        updated[1],
        updated[2],
        updated[3],
        updated[4],
        updated[5],
        updated[6],
        updated[7],
        updated[8],
        updated[9],
        updated[10],
        updated[11],
        updated[12],
        updated[13],
        updated[14],
        updated[15],
        updated[16],
        updated[17],
    )


def solution(mesh):
    placed = (
        P("fsdp", "seq", None),
        P("fsdp", None),
        P("fsdp", "seq", None),
        P(("seq", "fsdp"), None),
        P(("seq", "fsdp"), None),
        P(("seq", "fsdp"), None),
        P(("seq", "fsdp"), None),
        P(("seq", "fsdp"), None),
        P(("seq", "fsdp"), None),
        P(("seq", "fsdp"), None),
        P(("seq", "fsdp"), None),
        P(("seq", "fsdp"), None),
        P(("seq", "fsdp"), None),
        P(("seq", "fsdp"), None),
        P(("seq", "fsdp"), None),
        P(None, ("seq", "fsdp")),
        P(None, ("seq", "fsdp")),
        P(None, ("seq", "fsdp")),
        P(None, ("seq", "fsdp")),
        P(None, ("seq", "fsdp")),
        P(None, ("seq", "fsdp")),
    )
    return jax.shard_map(
        body,
        mesh=mesh,
        in_specs=placed,
        out_specs=(
            P("fsdp", "seq", None),
            P("fsdp", "seq", None),
            P(("seq", "fsdp"), None),
            P(("seq", "fsdp"), None),
            P(("seq", "fsdp"), None),
            P(("seq", "fsdp"), None),
            P(("seq", "fsdp"), None),
            P(("seq", "fsdp"), None),
            P(("seq", "fsdp"), None),
            P(("seq", "fsdp"), None),
            P(("seq", "fsdp"), None),
            P(("seq", "fsdp"), None),
            P(("seq", "fsdp"), None),
            P(("seq", "fsdp"), None),
            P(None, ("seq", "fsdp")),
            P(None, ("seq", "fsdp")),
            P(None, ("seq", "fsdp")),
            P(None, ("seq", "fsdp")),
            P(None, ("seq", "fsdp")),
            P(None, ("seq", "fsdp")),
        ),
        check_vma=False,
    )
```

profile of v0, /device:TPU:0, one launch (start us, length us, event | category | flops | bytes accessed | tf_op | source)
XLA Modules:
  0.0 3685.8 jit_solution(16151035694852974193)
XLA Ops:
  12.9 72.2 %all-gather.1 = bf16[32,64,10]{1,2,0:T(8,128)(2,1)S(1)} all-gather(bf16[1,64,10]{1,2,0:T(8,128)(2,1)S(1)} %convert_bitcast_fusion.1), channel_id=1, replica_groups=mesh['seq'=8,'fsdp'=4] {'seq','fsdp'}, dimensions={0}, use_global_device_ids=true | all-gather | bytes 42240 | tf_op jit(solution)/shard_map/all_gather | solution.py:204
  85.2 63.9 %all-gather = bf16[32,64,2]{1,2,0:T(2,128)(2,1)S(1)} all-gather(bf16[1,64,2]{1,2,0:T(2,128)(2,1)S(1)} %convert_bitcast_fusion.2), channel_id=1, replica_groups=mesh['seq'=8,'fsdp'=4] {'seq','fsdp'}, dimensions={0}, use_global_device_ids=true | all-gather | bytes 8448 | tf_op jit(solution)/shard_map/all_gather | solution.py:203
  151.0 19.3 all-gather.7.cloned.1.call-done
  170.3 11.7 fusion.46
  183.9 4.1 all-to-all-start
  188.1 49.8 %all-to-all-done = bf16[128,3,8,256]{3,0,1,2:T(8,128)(2,1)S(1)} async-done(((bf16[128,3,8,256]{3,0,1,2:T(8,128)(2,1)}), bf16[128,3,8,256]{3,0,1,2:T(8,128)(2,1)S(1)}, u32[]{:S(2)}, u32[]{:S(2)}) %all-to-all-start) | async-done | bytes 1572896 | tf_op jit(solution)/shard_map/all_to_all | solution.py:215
  240.4 28.6 while.75
  242.4 4.2 while.78
  247.2 3.5 while.79
  247.8 3.0 fusion.172
  252.9 8.3 while.78
  261.9 7.1 while.79
  262.4 3.0 fusion.172
  265.9 3.0 fusion.172
  270.9 3.8 reduce.2
  275.7 3.5 all-to-all-start.1
  280.3 27.3 all-to-all-done.1
  310.5 4.9 fusion.111
  315.7 159.4 %all-gather.11.cloned.1.call-done = bf16[2048,8192]{1,0:T(8,128)(2,1)} async-done(((bf16[64,8192]{1,0:T(8,128)(2,1)}), bf16[2048,8192]{1,0:T(8,128)(2,1)}) %all-gather.11.cloned.1.call-update) | async-done | bytes 33554448 | tf_op jit(solution)/shard_map/all_gather | solution.py:201
  475.1 17.2 convolution_add_fusion
  492.3 28.6 fusion.78
  520.9 1402.6 %reduce-scatter.5.cloned.1.call-done = f32[256,2048]{1,0:T(8,128)} async-done(((f32[8192,2048]{1,0:T(8,128)}), f32[256,2048]{1,0:T(8,128)}) %reduce-scatter.5.cloned.1.call-update) | async-done | bytes 2097168 | tf_op jit(solution)/shard_map/reduce_scatter | solution.py:255
  1923.6 8.3 add_multiply_fusion.2
  1931.9 195.1 %all-gather.13.cloned.1.call-done = bf16[8192,2048]{1,0:T(8,128)(2,1)} async-done(((bf16[256,2048]{1,0:T(8,128)(2,1)}), bf16[8192,2048]{1,0:T(8,128)(2,1)}) %all-gather.13.cloned.1.call-update) | async-done | bytes 33554448 | tf_op jit(solution)/shard_map/all_gather | solution.py:202
  2127.0 26.9 convert_reduce_fusion
  2153.8 19.6 multiply_reduce_fusion
  2176.1 6.3 convolution_convert_fusion
  2183.4 3.7 all-to-all-start.2
  2187.1 15.2 all-to-all-done.2
  2207.9 48.7 %while.77 = (s32[]{:T(128)}, f32[1024,4,64]{0,2,1:T(8,128)S(1)}, bf16[2,512,4,64]{1,3,2,0:T(8,128)(2,1)}, bf16[2,512,4,64]{1,3,2,0:T(8,128)(2,1)}, s32[2]{0:T(12...) while((s32[]{:T(128)}, f32[1024,4,64]{0,2,1:T(8,128)S(1)}, ...), condition=%wide.region_18.19_spmd.clone, body=%wide.region_15.18_spmd.clone.sunk | while | flops 687604736 | bytes 50939204 | solution.py:153
  2211.3 26.5 while.80
  2212.6 2.8 fusion.163
  2216.7 4.3 multiply_convert_fusion.6
  2225.6 2.8 fusion.163
  2229.6 4.3 multiply_convert_fusion.6
  2242.1 13.6 while.80
  2243.4 2.8 fusion.163
  2247.5 4.3 multiply_convert_fusion.6
  2263.4 4.5 all-to-all-start.3
  2268.0 8.2 fusion.92
  2276.2 25.3 fusion.102
  2301.5 15.4 all-to-all-done.3
  2316.9 3.0 copy.298
  2323.7 19.5 fusion.75
  2343.3 14.5 fusion.104
  2359.7 2.9 convert_reduce_fusion.2
  2363.7 87.6 %pad_maximum_fusion = f32[2048,16396]{1,0:T(8,128)} fusion(f32[2048,12]{1,0:T(8,128)S(1)} %bitcast.290, f32[2048,8192]{1,0:T(8,128)} %fusion.102, f32[2048,2048]{1,0:T(8,128)} %fusion.92, f32[2048,6144]{1,0:T(8,128)} %fusion.75), kind=kLoop, calls=%fused_computation.69 | loop fusion | flops 100737024 | bytes 268632064 | tf_op jit(solution)/shard_map/concatenate | solution.py:327
  2451.4 3.5 copy.304
  2456.2 3.0 copy.310
  2459.2 3.6 copy.305
  2467.8 4.1 copy.311
  2472.0 4.2 copy.309
  2476.2 24.4 fusion.56
  2500.5 1116.0 %reduce-scatter.7.cloned.1.call-done = f32[64,16396]{1,0:T(8,128)} async-done(((f32[2048,16396]{1,0:T(8,128)}), f32[64,16396]{1,0:T(8,128)}) %reduce-scatter.7.cloned.1.call-update) | async-done | bytes 4197392
  3620.2 8.9 add_multiply_fusion.1
  3629.1 3.2 copy.312
  3632.3 3.3 copy.313
  3635.6 3.5 copy.314
  3640.4 3.4 add_multiply_fusion.3
  3651.0 2.7 copy.331
  3653.7 11.3 add_multiply_fusion
  3665.0 3.8 copy.318
  3668.8 3.8 copy.319
  3672.6 3.8 copy.320
  (325 shorter events, 98.0 us)
Async XLA Ops:
  7.2 4.5 copy-start.10
  7.2 5.6 copy-start.38
  7.2 77.9 %copy-start.50 = (f32[2,64]{1,0:T(2,128)S(1)}, f32[2,64]{1,0:T(2,128)}, u32[]{:S(2)}) copy-start(f32[2,64]{1,0:T(2,128)} %param.46) | copy-start | bytes 1540
  7.2 142.6 %copy-start.4 = (bf16[1,128,2048]{2,1,0:T(8,128)(2,1)S(1)}, bf16[1,128,2048]{2,1,0:T(8,128)(2,1)}, u32[]{:S(2)}) copy-start(bf16[1,128,2048]{2,1,0:T(8,128)(2,1)} %param.31) | copy-start | bytes 1572868
  7.2 163.0 %all-gather.7.cloned.1.call-start = ((), (), s32[]{:S(2)}) async-start(), calls=%async_computation.6 | async-start | bytes 25952256 | tf_op jit(solution)/shard_map/all_gather | solution.py:199
  9.8 300.6 %all-gather.9.cloned.1.call-start = ((), (), s32[]{:S(2)}) async-start(), calls=%async_computation.7 | async-start | bytes 8650752 | tf_op jit(solution)/shard_map/all_gather | solution.py:200
  11.7 463.4 %all-gather.11.cloned.1.call-start = ((), (), s32[]{:S(2)}) async-start(), calls=%async_computation.8 | async-start | bytes 34603008 | tf_op jit(solution)/shard_map/all_gather | solution.py:201
  85.2 96.8 %copy-start.26 = (f32[2048,10]{0,1:T(8,128)}, f32[2048,10]{0,1:T(8,128)S(1)}, u32[]{:S(2)}) copy-start(f32[2048,10]{0,1:T(8,128)S(1)} %reshape.526) | copy-start | bytes 245764
  149.8 32.2 copy-start.29
  150.0 32.0 copy-start.33
  150.3 31.7 copy-start.54
  150.3 31.7 copy-start.43
  151.0 31.1 copy-start.20
  183.9 54.0 %all-to-all-start = ((bf16[128,3,8,256]{3,0,1,2:T(8,128)(2,1)}), bf16[128,3,8,256]{3,0,1,2:T(8,128)(2,1)S(1)}, u32[]{:S(2)}, u32[]{:S(2)}) async-start(bf16[128,3,8,256]{3,0,1,2:T(8,128)(2,1)} %copy.283), calls=%async_computation | async-start | bytes 3145728 | tf_op jit(solution)/shard_map/all_to_all | solution.py:215
  188.1 52.3 %copy-start.14 = (s32[1,1024]{1,0:T(1,128)S(1)}, s32[1,1024]{1,0:T(1,128)}, u32[]{:S(2)}) copy-start(s32[1,1024]{1,0:T(1,128)} %param.32) | copy-start | bytes 12292
  270.4 40.0 %copy-start.5 = (bf16[1,128,2048]{2,1,0:T(8,128)(2,1)S(1)}, bf16[1,128,2048]{2,1,0:T(8,128)(2,1)}, u32[]{:S(2)}) copy-start(bf16[1,128,2048]{2,1,0:T(8,128)(2,1)} %param.31) | copy-start | bytes 1572868
  270.4 40.0 %copy-start.37 = (f32[1,2048]{1,0:T(1,128)S(1)}, f32[1,2048]{1,0:T(1,128)}, u32[]{:S(2)}) copy-start(f32[1,2048]{1,0:T(1,128)} %get-tuple-element.976) | copy-start | bytes 24580
  275.7 32.0 all-to-all-start.1
  279.2 1644.4 %reduce-scatter.5.cloned.1.call-start = ((), (), s32[]{:S(2)}) async-start(), calls=%async_computation.10 | async-start | bytes 69206016 | tf_op jit(solution)/shard_map/reduce_scatter | solution.py:255
  310.4 5.0 copy-start.12
  310.4 164.6 %copy-start.22 = (f32[1,2048]{1,0:T(1,128)S(1)}, f32[1,2048]{1,0:T(1,128)}, u32[]{:S(2)}) copy-start(f32[1,2048]{1,0:T(1,128)} %get-tuple-element.980) | copy-start | bytes 24580
  310.5 164.6 %copy-start.27 = (f32[1,2048]{1,0:T(1,128)S(1)}, f32[1,2048]{1,0:T(1,128)}, u32[]{:S(2)}) copy-start(f32[1,2048]{1,0:T(1,128)} %get-tuple-element.974) | copy-start | bytes 24580
  315.4 1858.1 %copy-start.1 = (f32[128,2048]{1,0:T(8,128)}, f32[128,2048]{1,0:T(8,128)S(1)}, u32[]{:S(2)}) copy-start(f32[128,2048]{1,0:T(8,128)S(1)} %get-tuple-element.983) | copy-start | bytes 3145732
  315.4 1858.1 %copy-start.31 = (f32[128]{0:T(128)}, f32[128]{0:T(128)S(1)}, u32[]{:S(2)}) copy-start(f32[128]{0:T(128)S(1)} %broadcast_multiply_fusion) | copy-start | bytes 1540
  315.7 1857.8 %copy-start.35 = (f32[128]{0:T(128)}, f32[128]{0:T(128)S(1)}, u32[]{:S(2)}) copy-start(f32[128]{0:T(128)S(1)} %fusion.100) | copy-start | bytes 1540
  475.1 17.2 copy-start.15
  520.9 1606.1 %all-gather.13.cloned.1.call-start = ((), (), s32[]{:S(2)}) async-start(), calls=%async_computation.9 | async-start | bytes 34603008 | tf_op jit(solution)/shard_map/all_gather | solution.py:202
  2175.1 7.3 copy-start.48
  2183.4 18.9 all-to-all-start.2
  2216.6 4.8 copy-start
  2216.6 4.8 copy-start.25
  2229.6 4.8 copy-start
  2229.6 4.8 copy-start.25
  2247.4 4.8 copy-start
  2247.5 4.8 copy-start.25
  2260.8 7.2 copy-start.8
  2260.8 7.2 copy-start.13
  2260.8 7.2 copy-start.49
  2263.4 4.6 copy-start.16
  2263.4 53.6 %all-to-all-start.3 = ((bf16[1024,3,1,256]{3,1,2,0:T(4,128)(2,1)}), bf16[1024,3,1,256]{3,1,2,0:T(4,128)(2,1)}, u32[]{:S(2)}, u32[]{:S(2)}) async-start(bf16[1024,3,1,256]{3,1,2,0:T(4,128)(2,1)} %copy.297), calls=%async_computation.3 | async-start | bytes 4194304 | tf_op jit(solution)/shard_map/all_to_all | solution.py:299
  2267.8 8.3 copy-start.40
  2267.9 8.3 copy-start.2
  2267.9 8.3 copy-start.23
  2267.9 8.3 copy-start.28
  2267.9 8.3 copy-start.32
  2267.9 8.3 copy-start.36
  2267.9 1348.7 %reduce-scatter.7.cloned.1.call-start = ((), (), s32[]{:S(2)}) async-start(), calls=%async_computation.11 | async-start | bytes 139493376
  2343.3 14.5 copy-start.55
  2357.8 4.8 copy-start.9
  2357.8 5.4 copy-start.41
  2357.8 5.4 copy-start.42
  2451.4 4.8 copy-start.11
  2459.2 5.9 copy-start.24
  2472.0 4.2 copy-start.3
  2472.0 4.2 copy-start.47
  3632.3 6.8 slice-start.1
  3635.6 4.8 copy-start.17
  3643.8 7.2 slice-start.2
  3672.6 4.9 copy-start.51
  3672.6 4.9 copy-start.52
  3672.6 4.9 copy-start.53
  3672.6 5.5 copy-start.39
  3672.6 5.5 copy-start.45
  3672.6 5.4 copy-start.46
  (10 other events, 32.7 us)
Sparse Core Ops, SparseCore 0:
  11.5 158.7 all-gather.6
  173.7 94.2 all-gather.8
  271.4 203.6 all-gather.10
  521.0 1402.5 reduce-scatter.4
  1932.0 194.9 all-gather.12
  2451.5 1165.0 reduce-scatter.6
where the time goes:
time: 3690 us
  waiting for transfers between devices  3000 us (81%)
  matrix products  252 us (7%)
  other arithmetic  151 us (4%)
  blocking collectives  136 us (4%)
  local copies, waits for them, and re-layouts  103 us (3%)
    reduce_scatter x1, waiting for transfers between devices, body(): lax.psum_scatter(jnp.einsum('tf,td->fd', activated, upstream_rows, prefer...  1400 us
    unnamed x7, waiting for transfers between devices  1120 us
    all_gather x1, waiting for transfers between devices, body(): lax.all_gather(lowered[3], ('seq', 'fsdp'), axis=0, tiled=True)  195 us
    all_gather x1, waiting for transfers between devices, body(): lax.all_gather(lowered[2], ('seq', 'fsdp'), axis=0, tiled=True)  159 us
    concatenate x1, other arithmetic, body(): jnp.concatenate([mix_part, out_part, up_part, small_part], axis=1)  87.6 us
  transfers between devices with their start and end apart: 10, of which 9 were waited for; matrix products, arithmetic and copies ran while one was open for 4% of the time, Pallas kernels for 0%

commit v1 on v0

v1 whole, which is shorter than its diff:
```python
import functools
import math

import jax
import jax.numpy as jnp
from jax import lax
from jax.experimental import pallas as pl
from jax.experimental.pallas import tpu as pltpu
from jax.sharding import PartitionSpec as P

D = 2048
HEADS = 32
HD = 64
FF = 8192

epsilon = 1e-05
mom_decay = 0.5
avg_decay = 0.5
base_rate = 0.02
vector_rate = 0.1

BF16 = jnp.bfloat16
F32 = jnp.float32
MESH = pl.DeviceIdType.MESH


class Net:
    def __init__(self, send, recv, near):
        self.send, self.recv, self.near = send, recv, near
        self.used = self.near_used = 0
        self.later = []

    def take(self, count):
        first = self.used
        self.used += count
        return first

    def copy(self, slot, src, dst, dev):
        return pltpu.make_async_remote_copy(
            src_ref=src,
            dst_ref=dst,
            send_sem=self.send.at[slot],
            recv_sem=self.recv.at[slot],
            device_id=dev,
            device_id_type=MESH,
        )

    def local(self, src, dst):
        made = pltpu.make_async_copy(src, dst, self.near.at[self.near_used])
        self.near_used += 1
        made.start()
        return made


def when(cond, act):
    if cond is None:
        act()
    else:
        pl.when(cond)(act)


def greet(partners):
    barrier = pltpu.get_barrier_semaphore()
    for cond, dev in partners:
        when(
            cond,
            functools.partial(
                pl.semaphore_signal, barrier, inc=1, device_id=dev, device_id_type=MESH
            ),
        )
    count = sum(1 for cond, _ in partners if cond is None)
    for cond, _ in partners:
        if cond is not None:
            count = count + jnp.where(cond, 1, 0)
    pl.semaphore_wait(barrier, count)


class Roles:
    def __init__(self, axis, length, place, side, stride, pair):
        self.axis, self.length, self.p, self.q = axis, length, place, side
        self.stride, self.pair = stride, pair

    def index(self, p, q):
        return p * self.stride + q * self.pair

    def dev(self, p, q):
        return {self.axis: self.index(p, q)}

    def partners(self):
        return [
            (None, self.dev(self.p, 1 - self.q)),
            (self.p + 1 < self.length, self.dev(self.p + 1, self.q)),
            (self.p > 0, self.dev(self.p - 1, self.q)),
        ]


def line_of(axis):
    me, size = lax.axis_index(axis), lax.axis_size(axis)
    return Roles(axis, size // 2, me // 2, me % 2, 2, 1)


def both_of(axis):
    me, size = lax.axis_index(axis), lax.axis_size(axis)
    first = line_of(axis)
    if size != 4:
        return first, first
    return first, Roles(axis, 2, me % 2, me // 2, 1, 2)


def everyone(axis):
    me, size = lax.axis_index(axis), lax.axis_size(axis)
    return [(None, {axis: (me + o) % size}) for o in range(1, size)]


def gather(net, ro, src, place):
    n, p, q = ro.length, ro.p, ro.q
    right, left = net.take(n - 1), net.take(n - 1)
    over_r, over_l, over_own = net.take(n - 1), net.take(n - 1), net.take(1)
    other = ro.dev(p, 1 - q)
    at = lambda k: place(ro.index(k, q))
    across = lambda k: place(ro.index(k, 1 - q))
    ref = lambda j, k: src if j == 0 else at(k)
    go_right = lambda j: net.copy(right + j, ref(j, p - j), at(p - j), ro.dev(p + 1, q))
    go_left = lambda j: net.copy(left + j, ref(j, p + j), at(p + j), ro.dev(p - 1, q))
    pass_r = lambda j: net.copy(over_r + j - 1, at(p - j), at(p - j), other)
    pass_l = lambda j: net.copy(over_l + j - 1, at(p + j), at(p + j), other)
    own = net.copy(over_own, src, at(p), other)
    pl.when(p + 1 < n)(lambda: go_right(0).start())
    pl.when(p > 0)(lambda: go_left(0).start())
    own.start()
    yield
    for j in range(1, n):

        @pl.when(p - j >= 0)
        def _():
            net.copy(right + j - 1, at(p - j), at(p - j), other).wait_recv()
            if j < n - 1:
                pl.when(p + 1 < n)(lambda: go_right(j).start())
            pass_r(j).start()

        @pl.when(p + j < n)
        def _():
            net.copy(left + j - 1, at(p + j), at(p + j), other).wait_recv()
            if j < n - 1:
                pl.when(p > 0)(lambda: go_left(j).start())
            pass_l(j).start()

        yield
    net.copy(over_own, src, across(p), other).wait_recv()
    for j in range(1, n):

        @pl.when(p - j >= 0)
        def _():
            net.copy(over_r + j - 1, across(p - j), across(p - j), other).wait_recv()

        @pl.when(p + j < n)
        def _():
            net.copy(over_l + j - 1, across(p + j), across(p + j), other).wait_recv()

    def finish():
        own.wait_send()
        for j in range(n):
            if j < n - 1:
                pl.when((p - j >= 0) & (p + 1 < n))(lambda: go_right(j).wait_send())
                pl.when((p + j < n) & (p > 0))(lambda: go_left(j).wait_send())
            if j > 0:
                pl.when(p - j >= 0)(lambda: pass_r(j).wait_send())
                pl.when(p + j < n)(lambda: pass_l(j).wait_send())

    net.later.append(finish)


def add_rows(dst, srcs, step=16):
    def one(i, _):
        at = pl.ds(pl.multiple_of(i * step, step), step)
        total = srcs[0][at, :].astype(F32)
        for s in srcs[1:]:
            total = total + s[at, :].astype(F32)
        dst[at, :] = total.astype(dst.dtype)
        return 0

    lax.fori_loop(0, dst.shape[0] // step, one, 0)


def scatter_scratch(ro_length, rows, cols):
    return [pltpu.VMEM((ro_length, rows, cols), BF16)] + [
        pltpu.VMEM((ro_length - 1, rows, cols), BF16)
    ] * 4


def scatter(net, ro, part, result, room):
    sib, out_r, in_r, out_l, in_l = room
    n, p, q = ro.length, ro.p, ro.q
    right, left, pair = net.take(n - 1), net.take(n - 1), net.take(n)
    other = ro.dev(p, 1 - q)
    order = []
    for j in range(n):
        order += [d for d in (n - 1 - j, j) if d not in order]
    mine = lambda d: part(ro.index(d, q))
    swap = lambda d: net.copy(pair + d, part(ro.index(d, 1 - q)), sib.at[d], other)
    send_r = lambda j: net.copy(right + j, out_r.at[j], in_r.at[j], ro.dev(p + 1, q))
    send_l = lambda j: net.copy(left + j, out_l.at[j], in_l.at[j], ro.dev(p - 1, q))
    for d in order:
        swap(d).start()
    yield
    for j in range(n - 1):
        dr, dl = n - 1 - j, j

        @pl.when(p < dr)
        def _():
            swap(dr).wait_recv()

            @pl.when(p > 0)
            def _():
                send_r(j).wait_recv()
                add_rows(out_r.at[j], [mine(dr), sib.at[dr], in_r.at[j]])

            @pl.when(p == 0)
            def _():
                add_rows(out_r.at[j], [mine(dr), sib.at[dr]])

            send_r(j).start()

        @pl.when(p > dl)
        def _():
            swap(dl).wait_recv()

            @pl.when(p < n - 1)
            def _():
                send_l(j).wait_recv()
                add_rows(out_l.at[j], [mine(dl), sib.at[dl], in_l.at[j]])

            @pl.when(p == n - 1)
            def _():
                add_rows(out_l.at[j], [mine(dl), sib.at[dl]])

            send_l(j).start()

        yield
    from_r, from_l = n - 1 - p, p
    swap(p).wait_recv()

    @pl.when(p > 0)
    def _():
        send_r(from_r).wait_recv()

    @pl.when(p < n - 1)
    def _():
        send_l(from_l).wait_recv()

    @pl.when(p == 0)
    def _():
        add_rows(result, [mine(p), sib.at[p], in_l.at[from_l]])

    @pl.when(p == n - 1)
    def _():
        add_rows(result, [mine(p), sib.at[p], in_r.at[from_r]])

    if n > 2:

        @pl.when((p > 0) & (p < n - 1))
        def _():
            add_rows(result, [mine(p), sib.at[p], in_r.at[from_r], in_l.at[from_l]])

    def finish():
        for d in order:
            swap(d).wait_send()
        for j in range(n - 1):
            pl.when(p < n - 1 - j)(lambda: send_r(j).wait_send())
            pl.when(p > j)(lambda: send_l(j).wait_send())

    net.later.append(finish)


def exchange(net, axis, src, place):
    me, n = lax.axis_index(axis), lax.axis_size(axis)
    slots = net.take(n - 1)
    near = net.local(src(me), place(me))
    sent = []
    for o in range(1, n):
        to = (me + o) % n
        sent.append(net.copy(slots + o - 1, src(to), place(me), {axis: to}))
        sent[-1].start()
    yield
    near.wait()
    for o in range(1, n):
        at = (me + n - o) % n
        net.copy(slots + o - 1, src(at), place(at), {axis: at}).wait_recv()
    net.later.append(lambda: [s.wait_send() for s in sent])


def together(*gens):
    live = list(gens)
    while live:
        for g in list(live):
            try:
                next(g)
            except StopIteration:
                live.remove(g)
        if live:
            yield


def then(first, makers):
    yield from first
    yield from together(*[m() for m in makers])


def run(net, *gens):
    for _ in together(*gens):
        pass
    for act in net.later:
        act()


VM = pl.BlockSpec(memory_space=pltpu.VMEM)
HB = pl.BlockSpec(memory_space=pl.ANY)


def comm_call(slots, kernel, cid, ins, in_specs, outs, out_specs, room):
    return pl.pallas_call(
        kernel,
        out_shape=[jax.ShapeDtypeStruct(*o) for o in outs],
        in_specs=in_specs,
        out_specs=out_specs,
        scratch_shapes=[
            pltpu.SemaphoreType.DMA((slots,)),
            pltpu.SemaphoreType.DMA((slots,)),
            pltpu.SemaphoreType.DMA((8,)),
        ]
        + room,
        compiler_params=pltpu.CompilerParams(
            collective_id=cid, has_side_effects=True, vmem_limit_bytes=56 << 20
        ),
    )(*ins)


def pair_masks():
    lane = lax.broadcasted_iota(jnp.int32, (1, 2 * HD), 1)
    return [lane < HD, lane >= HD]


def block_scores(key_rows, query_block, start_row, first, slope):
    count, width = key_rows.shape[0], query_block.shape[0]
    raw = lax.dot_general(
        key_rows, query_block, (((1,), (1,)), ((), ())), preferred_element_type=F32
    )
    key_at = lax.broadcasted_iota(jnp.int32, (count, width), 0)
    query_at = lax.broadcasted_iota(jnp.int32, (1, width), 1) + first
    scores = raw - slope * (query_at - key_at).astype(F32)
    allowed = (key_at <= query_at) & (key_at >= start_row)
    return jnp.where(allowed, scores, -1e30)


def attend_kernel(block, slopes_ref, start_ref, q_ref, k_ref, v_ref, out_ref, lse_ref):
    length = q_ref.shape[0]
    pair = pl.program_id(0)
    for half, mask in enumerate(pair_masks()):
        keys = jnp.where(mask, k_ref[...], 0)
        turned = jnp.where(mask, v_ref[...], 0).T
        slope = slopes_ref[2 * pair + half]
        for first in range(0, length, block):
            here, upto = slice(first, first + block), first + block
            query_block = q_ref[here, :] * BF16(HD**-0.5)
            scores = block_scores(
                keys[:upto], query_block, start_ref[:, here], first, slope
            )
            top = jnp.max(scores, axis=0, keepdims=True)
            weights = jnp.exp(scores - top)
            total = jnp.sum(weights, axis=0, keepdims=True)
            lse_ref[0, half : half + 1, here] = top + jnp.log(total)
            probs = (weights * (1.0 / total)).astype(BF16)
            got = jnp.dot(turned[:, :upto], probs, preferred_element_type=F32).T
            if half == 0:
                out_ref[here, :] = got.astype(BF16)
            else:
                out_ref[here, :] = out_ref[here, :] + got.astype(BF16)


def attend_back_kernel(
    block, slopes_ref, start_ref, q_ref, k_ref, v_ref, o_ref, g_ref, lse_ref, dq_ref, dk_ref, dv_ref, dk, dv
):
    length = q_ref.shape[0]
    pair = pl.program_id(0)
    dk[...] = jnp.zeros_like(dk)
    dv[...] = jnp.zeros_like(dv)
    masks = pair_masks()
    for half, mask in enumerate(masks):
        keys = jnp.where(mask, k_ref[...], 0)
        values = jnp.where(mask, v_ref[...], 0)
        turned = keys.T * BF16(HD**-0.5)
        slope = slopes_ref[2 * pair + half]
        for first in range(0, length, block):
            here, upto = slice(first, first + block), first + block
            query_block = jnp.where(mask, q_ref[here, :], 0) * BF16(HD**-0.5)
            grad_block = jnp.where(mask, g_ref[here, :], 0)
            product = o_ref[here, :].astype(F32) * grad_block.astype(F32)
            delta = jnp.sum(product.T, axis=0, keepdims=True)
            scores = block_scores(
                keys[:upto], query_block, start_ref[:, here], first, slope
            )
            probs = jnp.exp(scores - lse_ref[0, half : half + 1, here])
            prob_grad = lax.dot_general(
                values[:upto], grad_block, (((1,), (1,)), ((), ())), preferred_element_type=F32
            )
            score_grad = (probs * (prob_grad - delta)).astype(BF16)
            dv[:upto, :] += jnp.dot(
                probs.astype(BF16), grad_block, preferred_element_type=F32
            )
            dk[:upto, :] += jnp.dot(score_grad, query_block, preferred_element_type=F32)
            got = jnp.dot(turned[:, :upto], score_grad, preferred_element_type=F32).T
            if half == 0:
                dq_ref[here, :] = got.astype(BF16)
            else:
                dq_ref[here, :] = dq_ref[here, :] + got.astype(BF16)
    dk_ref[...] = dk[...].astype(BF16)
    dv_ref[...] = dv[...].astype(BF16)


def attend_specs(length, pairs):
    column = lambda k: pl.BlockSpec((length, 2 * HD), lambda i, k=k: (0, k * pairs + i))
    fixed = [
        pl.BlockSpec(memory_space=pltpu.SMEM),
        pl.BlockSpec((1, length), lambda i: (0, 0)),
    ]
    lse = pl.BlockSpec((1, 2, length), lambda i: (i, 0, 0))
    return column, fixed, lse


ATTEND = pltpu.CompilerParams(vmem_limit_bytes=48 << 20)


def attend(mixed, start, slopes):
    length, pairs = mixed.shape[0], mixed.shape[1] // (6 * HD)
    column, fixed, lse = attend_specs(length, pairs)
    return pl.pallas_call(
        functools.partial(attend_kernel, min(256, length)),
        grid=(pairs,),
        in_specs=fixed + [column(0), column(1), column(2)],
        out_specs=[column(0), lse],
        out_shape=[
            jax.ShapeDtypeStruct((length, pairs * 2 * HD), BF16),
            jax.ShapeDtypeStruct((pairs, 2, length), F32),
        ],
        compiler_params=ATTEND,
    )(slopes, start, mixed, mixed, mixed)


def attend_back(mixed, attended, upstream, log_sums, start, slopes):
    length, pairs = mixed.shape[0], mixed.shape[1] // (6 * HD)
    column, fixed, lse = attend_specs(length, pairs)
    wide = jax.ShapeDtypeStruct((length, pairs * 2 * HD), BF16)
    return pl.pallas_call(
        functools.partial(attend_back_kernel, min(256, length)),
        grid=(pairs,),
        in_specs=fixed + [column(0), column(1), column(2), column(0), column(0), lse],
        out_specs=[column(0)] * 3,
        out_shape=[wide] * 3,
        scratch_shapes=[pltpu.VMEM((length, 2 * HD), F32)] * 2,
        compiler_params=ATTEND,
    )(slopes, start, mixed, mixed, mixed, attended, upstream, log_sums)


def layer_norm(values, gain_row, shift_row):
    centred = values - jnp.mean(values, axis=-1, keepdims=True)
    spread = jnp.mean(centred * centred, axis=-1, keepdims=True)
    return centred * lax.rsqrt(spread + epsilon) * gain_row + shift_row


def gelu_exact(values):
    return jax.nn.gelu(values, approximate=False)


def body(
    tokens,
    segments,
    cotangent,
    mix_weight,
    mix_moment,
    mix_average,
    out_weight,
    out_moment,
    out_average,
    up_weight,
    up_moment,
    up_average,
    down_weight,
    down_moment,
    down_average,
    norm_gains,
    gain_moment,
    gain_average,
    biases,
    bias_moment,
    bias_average,
):
    S, F = lax.axis_size("seq"), lax.axis_size("fsdp")
    owners = S * F
    s_at = lax.axis_index("seq")
    T = tokens.shape[1]
    L = T * S
    R = D // owners
    RD = FF // owners
    W = D // S
    U = FF // S
    heads = HEADS // S
    slots = 12 * max(S, F)
    call = functools.partial(comm_call, slots)

    head_ids = s_at * heads + jnp.arange(heads, dtype=jnp.int32) + 1
    slopes = jnp.exp2(-8.0 * head_ids.astype(F32) / HEADS)
    documents = segments[0]
    start = jnp.sum(documents[:, None] < documents[None, :], axis=0, dtype=jnp.int32)[None]

    mix_low = mix_weight.astype(BF16).reshape(R, 3, S, W).transpose(2, 0, 1, 3).reshape(S, R, 3 * W)
    up_low = up_weight.astype(BF16).reshape(R, S, U).transpose(1, 0, 2)
    out_low = out_weight.astype(BF16)
    down_low = down_weight.astype(BF16)
    small = jnp.concatenate([norm_gains, biases], axis=0).astype(BF16).astype(F32)
    small = jnp.pad(small, ((0, 4), (0, 128 - R)))

    def first_kernel(tok, mix, out, vec, tok_f, mix_f, out_f, vec_f, send, recv, near):
        net = Net(send, recv, near)
        seq, sides = line_of("seq"), both_of("fsdp")
        s, f = lax.axis_index("seq"), lax.axis_index("fsdp")
        greet(everyone("seq") + everyone("fsdp"))
        owned = [
            net.local(tok, tok_f.at[s]),
            net.local(out, out_f.at[f]),
        ]
        vec_own = net.local(vec, vec_f.at[s, f])

        def mix_half(k):
            at = pl.ds(k * (S // 2), S // 2)
            return lambda: gather(net, sides[k], mix_f.at[at, f], lambda i: mix_f.at[at, i])

        def out_half(k):
            at = pl.ds(k * (D // 2), D // 2)
            return gather(net, sides[k], out.at[:, at], lambda i: out_f.at[i, :, at])

        def vec_next():
            vec_own.wait()
            return gather(net, sides[0], vec_f.at[:, f], lambda i: vec_f.at[:, i])

        run(
            net,
            then(
                exchange(net, "seq", lambda i: mix.at[i], lambda i: mix_f.at[i, f]),
                [mix_half(0), mix_half(1)],
            ),
            then(gather(net, seq, vec, lambda i: vec_f.at[i, f]), [vec_next]),
            out_half(0),
            out_half(1),
            gather(net, seq, tok, lambda i: tok_f.at[i]),
        )
        for o in owned:
            o.wait()

    tok_full, mix_full, out_full, vec_full = call(
        first_kernel,
        1,
        (tokens[0], mix_low, out_low, small),
        [HB] * 4,
        [
            ((S, T, D), BF16),
            ((S, F, R, 3 * W), BF16),
            ((F, R, D), BF16),
            ((S, F, 16, 128), F32),
        ],
        [HB] * 4,
        [],
    )
    vectors = vec_full[:, :, :12, :R].transpose(2, 0, 1, 3).reshape(12, D)
    gain_values, bias_values = vectors[:2], vectors[2:]
    mine = lambda row, width: lax.dynamic_slice_in_dim(row.reshape(-1), s_at * width, width)
    mix_own = mix_full.reshape(D, 3 * W)
    out_own = out_full.reshape(W, D)

    normed = layer_norm(
        tok_full.reshape(L, D).astype(F32), gain_values[0], bias_values[0]
    ).astype(BF16)
    mix_bias = jnp.concatenate(
        [mine(bias_values[1], W), jnp.zeros((W,), F32), mine(bias_values[2], W)]
    )
    mixed = (jnp.dot(normed, mix_own, preferred_element_type=F32) + mix_bias).astype(BF16)
    attended, log_sums = attend(mixed, start, slopes)
    out_part = jnp.dot(attended, out_own, preferred_element_type=F32).astype(BF16)

    def second_kernel(part, cot, up, down, total, cot_f, up_r, down_f, send, recv, near, *room):
        net = Net(send, recv, near)
        seq, sides = line_of("seq"), both_of("fsdp")
        s, f = lax.axis_index("seq"), lax.axis_index("fsdp")
        greet(everyone("seq") + everyone("fsdp"))
        owned = [net.local(cot, cot_f.at[s]), net.local(down, down_f.at[f])]

        def down_half(k):
            at = pl.ds(k * (RD // 2), RD // 2)
            return gather(net, sides[k], down.at[at], lambda i: down_f.at[i, at])

        run(
            net,
            scatter(net, seq, lambda i: part.at[i], total, room),
            down_half(0),
            down_half(1),
            gather(net, seq, cot, lambda i: cot_f.at[i]),
            exchange(net, "seq", lambda i: up.at[i], lambda i: up_r.at[i]),
        )
        for o in owned:
            o.wait()

    attn_sum, cot_full, up_mid, down_full = call(
        second_kernel,
        2,
        (out_part.reshape(S, T, D), cotangent[0], up_low, down_low),
        [VM, HB, HB, HB],
        [((T, D), F32), ((S, T, D), BF16), ((S, R, U), BF16), ((F, RD, D), BF16)],
        [VM, HB, HB, HB],
        scatter_scratch(S // 2, T, D),
    )
    row_values = tokens[0].astype(F32)
    hidden_in = row_values + attn_sum + bias_values[3]
    normed_two = layer_norm(hidden_in, gain_values[1], bias_values[4]).astype(BF16)

    def third_kernel(rows, up, rows_f, up_f, send, recv, near):
        net = Net(send, recv, near)
        seq, sides = line_of("seq"), both_of("fsdp")
        s, f = lax.axis_index("seq"), lax.axis_index("fsdp")
        greet(seq.partners() + everyone("fsdp"))
        owned = [net.local(rows, rows_f.at[s]), net.local(up, up_f.at[:, f])]

        def up_half(k):
            at = pl.ds(k * (S // 2), S // 2)
            return gather(net, sides[k], up.at[at], lambda i: up_f.at[at, i])

        run(
            net,
            up_half(0),
            up_half(1),
            gather(net, seq, rows, lambda i: rows_f.at[i]),
        )
        for o in owned:
            o.wait()

    two_full, up_full = call(
        third_kernel,
        3,
        (normed_two, up_mid),
        [HB, HB],
        [((S, T, D), BF16), ((S, F, R, U), BF16)],
        [HB, HB],
        [],
    )
    two_full = two_full.reshape(L, D)
    cot_full = cot_full.reshape(L, D)
    up_own = up_full.reshape(D, U)
    down_own = down_full.reshape(U, D)
    pre_act = jnp.dot(two_full, up_own, preferred_element_type=F32) + mine(bias_values[6:10], U)
    activated = gelu_exact(pre_act).astype(BF16)
    result_part = jnp.dot(activated, down_own, preferred_element_type=F32).astype(BF16)
    act_grad = jnp.einsum("td,fd->tf", cot_full, down_own, preferred_element_type=F32)
    pre_grad = jax.vjp(gelu_exact, pre_act)[1](act_grad)[0].astype(BF16)
    two_grad_part = jnp.einsum("tf,cf->tc", pre_grad, up_own, preferred_element_type=F32)
    down_part = jnp.einsum("tf,td->fd", activated, cot_full, preferred_element_type=F32)
    up_part = jnp.einsum("tc,tf->cf", two_full, pre_grad, preferred_element_type=F32)

    def fourth_kernel(part, grad, total, share, send, recv, near, *room):
        net = Net(send, recv, near)
        seq, sides = line_of("seq"), both_of("fsdp")
        greet(seq.partners() + everyone("fsdp"))

        def half(k):
            at = pl.ds(k * (D // 2), D // 2)
            return scatter(
                net, sides[k], lambda i: grad.at[i, :, at], share.at[:, at], room[5 + 5 * k : 10 + 5 * k]
            )

        run(net, scatter(net, seq, lambda i: part.at[i], total, room[:5]), half(0), half(1))

    two_grad, down_share = call(
        fourth_kernel,
        4,
        (two_grad_part.astype(BF16).reshape(S, T, D), down_part.astype(BF16).reshape(F, RD, D)),
        [VM, VM],
        [((T, D), F32), ((RD, D), F32)],
        [VM, VM],
        scatter_scratch(S // 2, T, D) + 2 * scatter_scratch(F // 2, RD, D // 2),
    )
    upstream_float = cotangent[0].astype(F32)
    second_pull = jax.vjp(layer_norm, hidden_in, gain_values[1], bias_values[4])[1]
    hidden_part, gain_two_gradient, shift_two_gradient = second_pull(two_grad)
    hidden_gradient = upstream_float + hidden_part
    hidden_low = hidden_gradient.astype(BF16)

    def fifth_kernel(rows, part, grad, rows_f, total, share, send, recv, near, *room):
        net = Net(send, recv, near)
        seq, sides = line_of("seq"), both_of("fsdp")
        s = lax.axis_index("seq")
        greet(seq.partners() + everyone("fsdp"))
        own = net.local(rows, rows_f.at[s])

        def half(k):
            at = pl.ds(k * (U // 2), U // 2)
            return scatter(
                net, sides[k], lambda i: grad.at[i, :, at], share.at[:, at], room[5 + 5 * k : 10 + 5 * k]
            )

        run(
            net,
            gather(net, seq, rows, lambda i: rows_f.at[i]),
            scatter(net, seq, lambda i: part.at[i], total, room[:5]),
            half(0),
            half(1),
        )
        own.wait()

    hidden_full, result_sum, up_mid_grad = call(
        fifth_kernel,
        5,
        (
            hidden_low,
            result_part.reshape(S, T, D),
            up_part.astype(BF16).reshape(S, F, R, U).transpose(1, 0, 2, 3).reshape(F, S * R, U),
        ),
        [HB, VM, VM],
        [((S, T, D), BF16), ((T, D), F32), ((S * R, U), BF16)],
        [HB, VM, VM],
        scatter_scratch(S // 2, T, D) + 2 * scatter_scratch(F // 2, S * R, U // 2),
    )
    output = (hidden_in + result_sum + bias_values[5]).astype(BF16)[None]
    hidden_full = hidden_full.reshape(L, D)
    attn_grad = jnp.einsum(
        "td,cd->tc", hidden_full, out_own, preferred_element_type=F32
    ).astype(BF16)
    query_grad, key_grad, value_grad = attend_back(
        mixed, attended, attn_grad, log_sums, start, slopes
    )
    mixed_grad = jnp.concatenate([query_grad, key_grad, value_grad], axis=1)
    one_grad_part = jnp.einsum("te,ce->tc", mixed_grad, mix_own, preferred_element_type=F32)
    out_grad = jnp.einsum("tc,td->cd", attended, hidden_full, preferred_element_type=F32)
    mix_grad = jnp.einsum("tc,te->ce", normed, mixed_grad, preferred_element_type=F32)

    def sixth_kernel(
        part, mix, out, up, total, mix_s, out_s, up_s, send, recv, near, mix_r, *room
    ):
        net = Net(send, recv, near)
        seq, sides = line_of("seq"), both_of("fsdp")
        greet(everyone("seq") + everyone("fsdp"))
        C = S * R // 2

        def mix_half(k):
            at = pl.ds(k * C, C)
            return scatter(
                net, sides[k], lambda i: mix.at[i, at], mix_r.at[at], room[5 + 5 * k : 10 + 5 * k]
            )

        def out_half(k):
            at = pl.ds(k * (D // 2), D // 2)
            return scatter(
                net, sides[k], lambda i: out.at[i, :, at], out_s.at[:, at], room[15 + 5 * k : 20 + 5 * k]
            )

        run(
            net,
            then(
                together(mix_half(0), mix_half(1)),
                [
                    lambda: exchange(
                        net, "seq", lambda i: mix_r.at[pl.ds(i * R, R)], lambda i: mix_s.at[i]
                    )
                ],
            ),
            scatter(net, seq, lambda i: part.at[i], total, room[:5]),
            exchange(net, "seq", lambda i: up.at[i], lambda i: up_s.at[i]),
            out_half(0),
            out_half(1),
        )

    one_grad, mix_share, out_share, up_share = call(
        sixth_kernel,
        6,
        (
            one_grad_part.astype(BF16).reshape(S, T, D),
            mix_grad.astype(BF16)
            .reshape(S, F, R, 3 * W)
            .transpose(1, 0, 2, 3)
            .reshape(F, S * R, 3 * W),
            out_grad.astype(BF16).reshape(F, R, D),
            up_mid_grad.reshape(S, R, U),
        ),
        [VM, VM, VM, HB],
        [((T, D), F32), ((S, R, 3 * W), BF16), ((R, D), F32), ((S, R, U), BF16)],
        [VM, HB, VM, HB],
        [pltpu.VMEM((S * R, 3 * W), BF16)]
        + scatter_scratch(S // 2, T, D)
        + 2 * scatter_scratch(F // 2, S * R // 2, 3 * W)
        + 2 * scatter_scratch(F // 2, R, D // 2),
    )
    first_pull = jax.vjp(layer_norm, row_values, gain_values[0], bias_values[0])[1]
    rows_part, gain_one_gradient, shift_one_gradient = first_pull(one_grad)
    tokens_grad = (hidden_gradient + rows_part).astype(BF16)[None]

    def spread(row, count):
        return lax.dynamic_update_slice_in_dim(
            jnp.zeros((count * S * row.shape[0] // count,), F32), row, s_at * row.shape[0], 0
        ).reshape(count, D)

    mixed_sum = jnp.sum(mixed_grad.astype(F32), axis=0)
    small_gradient = jnp.concatenate(
        [
            gain_one_gradient[None],
            gain_two_gradient[None],
            shift_one_gradient[None],
            spread(mixed_sum[:W], 1),
            spread(mixed_sum[2 * W :], 1),
            jnp.sum(hidden_gradient, axis=0)[None],
            shift_two_gradient[None],
            jnp.sum(upstream_float, axis=0)[None],
            spread(jnp.sum(pre_grad.astype(F32), axis=0), 4),
        ],
        axis=0,
    )
    small_gradient = jnp.pad(
        small_gradient.reshape(12, S, F, R).transpose(1, 2, 0, 3),
        ((0, 0), (0, 0), (0, 4), (0, 128 - R)),
    )

    def last_kernel(vec, total, send, recv, near, got, mid, got_two):
        net = Net(send, recv, near)
        greet(everyone("seq") + everyone("fsdp"))
        for _ in exchange(net, "seq", lambda i: vec.at[i], lambda i: got.at[i]):
            pass
        mid[...] = jnp.sum(got[...], axis=0)
        for _ in exchange(net, "fsdp", lambda i: mid.at[i], lambda i: got_two.at[i]):
            pass
        total[...] = jnp.sum(got_two[...], axis=0)
        run(net)

    (small_share,) = call(
        last_kernel,
        7,
        (small_gradient,),
        [VM],
        [((16, 128), F32)],
        [VM],
        [
            pltpu.VMEM((S, F, 16, 128), F32),
            pltpu.VMEM((F, 16, 128), F32),
            pltpu.VMEM((F, 16, 128), F32),
        ],
    )
    mix_final = mix_share.astype(F32).reshape(S, R, 3, W).transpose(1, 2, 0, 3).reshape(R, 3 * D)
    up_final = up_share.astype(F32).transpose(1, 0, 2).reshape(R, FF)
    step_rate = base_rate / math.sqrt(owners * T)
    vector_step = vector_rate / math.sqrt(owners * T)
    rate_list = (step_rate, step_rate, step_rate, step_rate, vector_step, vector_step)
    masters = (mix_weight, out_weight, up_weight, down_weight, norm_gains, biases)
    shares = (mix_final, out_share, up_final, down_share, small_share[:2, :R], small_share[2:12, :R])
    moments = (mix_moment, out_moment, up_moment, down_moment, gain_moment, bias_moment)
    averages = (mix_average, out_average, up_average, down_average, gain_average, bias_average)
    updated = []
    for master, moment, average, share, rate in zip(masters, moments, averages, shares, rate_list):
        new_moment = mom_decay * moment + share
        new_weight = master - rate * (share + mom_decay * new_moment)
        new_average = avg_decay * average + (1.0 - avg_decay) * new_weight
        updated += [new_moment, new_weight, new_average]
    return (output, tokens_grad, *updated)


def solution(mesh):
    rows = P("fsdp", "seq", None)
    param = P(("seq", "fsdp"), None)
    vector = P(None, ("seq", "fsdp"))
    return jax.shard_map(
        body,
        mesh=mesh,
        in_specs=(rows, P("fsdp", None), rows) + (param,) * 12 + (vector,) * 6,
        out_specs=(rows, rows) + (param,) * 12 + (vector,) * 6,
        check_vma=False,
    )
```

time: 3690 us -> 684 us (0.19)
  waiting for transfers between devices: 3000 us -> 0 us
  Pallas kernels: 0 us -> 526 us
  matrix products: 252 us -> 75.5 us
  blocking collectives: 136 us -> 0 us
  other arithmetic: 151 us -> 51.4 us
  local copies, waits for them, and re-layouts: 103 us -> 22.3 us
    reduce_scatter x1 -> x0, waiting for transfers between devices: 1400 us -> none  [body(): lax.psum_scatter(jnp.einsum('tf,td->fd', activated, upstream_rows, prefer...]
    unnamed x7 -> x0, waiting for transfers between devices: 1120 us -> none
    pallas_call x0 -> x9, Pallas kernels: none -> 526 us  [the longest x7 506 us: comm_call(): pl.pallas_call(kernel, out_shape=[jax.ShapeDtypeStruct(*o) for o in outs]...]
    all_gather x4 -> x0, waiting for transfers between devices: 374 us -> none  [the longest x1 195 us: body(): lax.all_gather(lowered[3], ('seq', 'fsdp'), axis=0, tiled=True)]
    dot_general x33 -> x12, matrix products: 252 us -> 75.5 us  [the longest x1 17.7 us: body(): jnp.einsum('td,fd->tf', cot_full, down_own, preferred_element_type=F32)]
    all_gather x2 -> x0, blocking collectives: 136 us -> none  [the longest x1 72.2 us: body(): lax.all_gather(lowered[5], ('seq', 'fsdp'), axis=1, tiled=True)]
    all_to_all x4 -> x0, waiting for transfers between devices: 108 us -> none  [the longest x1 49.8 us: body(): lax.all_to_all(mixed_rows.reshape(tok_count, 3, groups, width_local), 'se...]
    concatenate x2 -> x1, other arithmetic: 87.6 us -> 0.01 us  [body(): jnp.concatenate([mine(bias_values[1], W), jnp.zeros((W,), F32), mine(bias...]
  transfers between devices with their start and end apart: 10 -> 0, of which waited for: 9 -> 0; matrix products, arithmetic and copies ran while one was open for 4% -> 0% of each run, Pallas kernels for 0% -> 0%
where the time goes in v1:
time: 684 us; the launch traced here: 677 us
  Pallas kernels  526 us (77%)
  matrix products  75.5 us (11%)
  other arithmetic  51.4 us (8%)
  local copies, waits for them, and re-layouts  22.3 us (3%)
    pallas_call x7, Pallas kernels, comm_call(): pl.pallas_call(kernel, out_shape=[jax.ShapeDtypeStruct(*o) for o in outs]...  506 us
    dot_general x1, matrix products, body(): jnp.einsum('td,fd->tf', cot_full, down_own, preferred_element_type=F32)  17.7 us
    add x6, other arithmetic, body(): new_average = avg_decay * average + (1.0 - avg_decay) * new_weight  16.4 us

profile of v1, /device:TPU:0, one launch (start us, length us, event | category | flops | bytes accessed | tf_op | source)
XLA Modules:
  0.0 676.9 jit_solution(6539391649451661918)
XLA Ops:
  0.7 1.5 convert_element_type.108
  2.8 1.7 reshape.293.mix
  4.5 0.7 convert_element_type.109.out
  5.2 0.6 fusion.27.vec
  5.8 77.4 %shard_map.356 = (bf16[8,128,2048]{2,1,0:T(8,128)(2,1)}, bf16[8,4,64,768]{3,2,1,0:T(8,128)(2,1)}, bf16[4,64,2048]{2,1,0:T(8,128)(2,1)}, f32[8,4,16,128]{3,2,1,0:T(8,128)}) custom-call(bf16[128,2048]{1,0:T(8,128)(2,1)} %bitcast.118, bf16[8,64,768]{2,1,0:T(8,128)(2,1)} %reshape.293.mix, bf16[64,2048]{1,0:T(8,128)(2,1)} %convert_element_type.109.out, ...), custom_call_target="tpu_custom_call" | custom-call | tf_op jit(solution)/shard_map/pallas_call | solution.py:321
  83.2 3.0 convert_reduce_fusion
  86.7 1.2 multiply_reduce_fusion
  87.9 0.9 slice_reduce_fusion
  89.0 4.6 add_convert_fusion
  94.0 6.6 add_convert_fusion.2.q_ref.k_ref.v_ref
  100.6 0.5 convert_reduce_fusion.2
  101.1 10.0 %shard_map.357 = (bf16[1024,256]{1,0:T(8,128)(2,1)S(1)}, f32[2,2,1024]{2,1,0:T(2,128)S(1)}) custom-call(f32[4]{0:T(128)S(1)} %multiply_exponential_fusion.slopes_ref, s32[1,1024]{1,0:T(1,128)S(1)} %bitcast.114, bf16[1024,768]{1,0:T(8,128)(2,1)S(1)} %add_convert_fusion.2.q_ref.k_ref.v_ref, bf16[1024,768]{1,0:T(8,128)(2,1)S(1)} %add_convert_fusion.2.q_ref.k_ref.v_ref, ...), custom_call_target="tpu_custom_call" | custom-call | tf_op jit(solution)/shard_map/pallas_call | solution.py:436
  111.1 3.2 convolution_convert_fusion
  114.5 1.1 copy.74
  115.6 0.8 copy-done.5
  116.3 1.1 convert_element_type.116.down
  117.5 109.7 %shard_map.358 = (f32[128,2048]{1,0:T(8,128)}, bf16[8,128,2048]{2,1,0:T(8,128)(2,1)}, bf16[8,64,1024]{2,1,0:T(8,128)(2,1)}, bf16[4,256,2048]{2,1,0:T(8,128)(2,1)}) custom-call(bf16[8,128,2048]{2,1,0:T(8,128)(2,1)} %bitcast.116, bf16[128,2048]{1,0:T(8,128)(2,1)} %bitcast.124, bf16[8,64,1024]{2,1,0:T(8,128)(2,1)} %bitcast.133, ...), custom_call_target="tpu_custom_call" | custom-call | tf_op jit(solution)/shard_map/pallas_call | solution.py:321
  227.3 1.6 fusion.38
  229.3 1.0 add_convert_fusion.5.rows
  230.4 54.5 %shard_map.359 = (bf16[8,128,2048]{2,1,0:T(8,128)(2,1)}, bf16[8,4,64,1024]{3,2,1,0:T(8,128)(2,1)}) custom-call(bf16[128,2048]{1,0:T(8,128)(2,1)} %add_convert_fusion.5.rows, bf16[8,64,1024]{2,1,0:T(8,128)(2,1)} %get-tuple-element.50.up), custom_call_target="tpu_custom_call" | custom-call | tf_op jit(solution)/shard_map/pallas_call | solution.py:321
  284.8 9.9 %fusion.41 = f32[1024,1024]{1,0:T(8,128)} fusion(bf16[1024,2048]{1,0:T(8,128)(2,1)} %bitcast.153, bf16[2048,1024]{1,0:T(8,128)(2,1)} %bitcast.149), kind=kOutput, calls=%fused_computation.129 | convolution fusion | flops 4294967296 | bytes 12582912 | tf_op jit(solution)/shard_map/dot_general | solution.py:657
  294.9 17.7 %convert_reduce_fusion.1 = (f32[1024]{0:T(1024)S(1)}, bf16[1024,1024]{1,0:T(8,128)(2,1)S(1)}, f32[1024,1024]{1,0:T(8,128)S(1)}) fusion(f32[1024,1024]{1,0:T(8,128)} %fusion.41, f32[1024]{0:T(1024)S(1)} %dynamic_slice.11, bf16[1024,2048]{1,0:T(8,128)(2,1)} %bitcast.145, bf16[1024,2048]{1,0:T(8,128)(2,1)} %bitcast.147), kind=kOutput, calls=%fused_computation.10 | convolution fusion | flops 4373609472 | bytes 18882560 | tf_op jit(solution)/shard_map/td,fd->tf/dot_general | solution.py:660
  312.6 4.9 convolution_convert_fusion.2
  317.6 2.6 copy.63
  320.2 1.1 copy-done.9
  321.3 1.2 multiply_convert_fusion
  322.4 1.0 copy-done.31
  323.5 6.1 convolution_convert_fusion.3
  329.5 6.2 convolution_convert_fusion.4
  335.8 6.4 convolution_convert_fusion.5
  342.1 62.2 %shard_map.360 = (f32[128,2048]{1,0:T(8,128)}, f32[256,2048]{1,0:T(8,128)}) custom-call(bf16[8,128,2048]{2,1,0:T(8,128)(2,1)} %bitcast.131, bf16[4,256,2048]{2,1,0:T(8,128)(2,1)} %bitcast.130), custom_call_target="tpu_custom_call" | custom-call | tf_op jit(solution)/shard_map/pallas_call | solution.py:321
  404.4 1.7 multiply_reduce_fusion.1
  406.1 1.6 fusion.37
  407.7 1.0 fusion.33.rows
  408.7 82.5 %shard_map.361 = (bf16[8,128,2048]{2,1,0:T(8,128)(2,1)}, f32[128,2048]{1,0:T(8,128)}, bf16[512,1024]{1,0:T(8,128)(2,1)}) custom-call(bf16[128,2048]{1,0:T(8,128)(2,1)} %fusion.33.rows, bf16[8,128,2048]{2,1,0:T(8,128)(2,1)} %bitcast.128, bf16[4,512,1024]{2,1,0:T(8,128)(2,1)} %bitcast.117), custom_call_target="tpu_custom_call" | custom-call | tf_op jit(solution)/shard_map/pallas_call | solution.py:321
  491.2 3.5 convolution_convert_fusion.8.g_ref
  494.7 10.0 %shard_map.362 = (bf16[1024,256]{1,0:T(8,128)(2,1)S(1)}, bf16[1024,256]{1,0:T(8,128)(2,1)S(1)}, bf16[1024,256]{1,0:T(8,128)(2,1)S(1)}) custom-call(f32[4]{0:T(128)S(1)} %multiply_exponential_fusion.slopes_ref, s32[1,1024]{1,0:T(1,128)S(1)} %bitcast.115, bf16[1024,768]{1,0:T(8,128)(2,1)S(1)} %add_convert_fusion.2.q_ref.k_ref.v_ref, ...), custom_call_target="tpu_custom_call" | custom-call | tf_op jit(solution)/shard_map/pallas_call | solution.py:453
  504.8 1.9 fusion.3
  506.7 3.8 convolution_convert_fusion.6
  510.5 2.0 copy.64
  512.5 1.3 copy-done.33
  513.8 2.2 convolution_convert_fusion.7
  516.0 5.0 convolution_convert_fusion.1
  521.0 104.3 %shard_map.363 = (f32[128,2048]{1,0:T(8,128)}, bf16[8,64,768]{2,1,0:T(8,128)(2,1)}, f32[64,2048]{1,0:T(8,128)}, bf16[8,64,1024]{2,1,0:T(8,128)(2,1)}) custom-call(bf16[8,128,2048]{2,1,0:T(8,128)(2,1)} %bitcast.129, bf16[4,512,768]{2,1,0:T(8,128)(2,1)} %bitcast.119, bf16[4,64,2048]{2,1,0:T(8,128)(2,1)} %bitcast.138, bf16[8,64,1024]{2,1,0:T(8,128)(2,1)} %bitcast.137), custom_call_target="tpu_custom_call" | custom-call | tf_op jit(solution)/shard_map/pallas_call | solution.py:321
  625.4 1.6 fusion.35
  627.1 1.8 fusion.17
  628.8 2.7 convert_reduce_fusion.5
  632.2 0.5 broadcast.416
  632.7 0.7 reduce.40
  633.5 0.7 reduce.41
  635.1 0.7 pad.12.vec
  635.9 15.2 %shard_map.364 = f32[16,128]{1,0:T(8,128)} custom-call(f32[8,4,16,128]{3,2,1,0:T(8,128)} %pad.12.vec), custom_call_target="tpu_custom_call" | custom-call | tf_op jit(solution)/shard_map/pallas_call | solution.py:321
  651.1 1.3 add_multiply_fusion.4
  652.4 1.3 add_multiply_fusion.5
  653.6 1.5 convert_bitcast_fusion
  655.4 3.3 add_multiply_fusion.1
  658.7 2.5 reshape.330
  661.3 0.9 copy.65
  662.2 0.5 copy.71
  663.1 0.5 copy-done.15
  663.6 2.7 add_multiply_fusion.2
  666.4 1.3 add_multiply_fusion.3
  667.7 2.1 fusion.19
  669.9 6.5 add_multiply_fusion
  (122 shorter events, 5.0 us)
Async XLA Ops:
  0.7 3.8 copy-start.12
  0.7 4.6 copy-start.23
  0.7 4.6 copy-start.27
  83.2 3.5 copy-start
  83.2 4.7 copy-start.21
  94.0 6.6 copy-start.24
  100.6 10.6 %copy-start.16 = (bf16[4,64,2048]{2,1,0:T(8,128)(2,1)S(1)}, bf16[4,64,2048]{2,1,0:T(8,128)(2,1)}, u32[]{:S(2)}) copy-start(bf16[4,64,2048]{2,1,0:T(8,128)(2,1)} %get-tuple-element.48) | copy-start | bytes 3145732
  111.1 3.3 copy-start.3
  114.4 2.0 copy-start.5
  294.9 17.7 %copy-start.34 = (bf16[8,128,2048]{2,1,0:T(8,128)(2,1)S(1)}, bf16[8,128,2048]{2,1,0:T(8,128)(2,1)}, u32[]{:S(2)}) copy-start(bf16[8,128,2048]{2,1,0:T(8,128)(2,1)} %get-tuple-element.51) | copy-start | bytes 12582916
  317.6 3.7 copy-start.9
  321.3 2.2 copy-start.31
  323.5 6.1 copy-start.30
  329.5 6.2 copy-start.32
  404.4 3.3 copy-start.8
  408.7 82.5 %copy-start.17 = (bf16[4,64,2048]{2,1,0:T(8,128)(2,1)S(1)}, bf16[4,64,2048]{2,1,0:T(8,128)(2,1)}, u32[]{:S(2)}) copy-start(bf16[4,64,2048]{2,1,0:T(8,128)(2,1)} %get-tuple-element.48) | copy-start | bytes 3145732
  494.7 10.1 %copy-start.1 = (bf16[8,128,2048]{2,1,0:T(8,128)(2,1)S(1)}, bf16[8,128,2048]{2,1,0:T(8,128)(2,1)}, u32[]{:S(2)}) copy-start(bf16[8,128,2048]{2,1,0:T(8,128)(2,1)} %get-tuple-element.44) | copy-start | bytes 12582916
  510.4 3.3 copy-start.33
  512.5 3.5 copy-start.35
  521.0 104.3 %copy-start.2 = (bf16[1,128,2048]{2,1,0:T(8,128)(2,1)S(1)}, bf16[1,128,2048]{2,1,0:T(8,128)(2,1)}, u32[]{:S(2)}) copy-start(bf16[1,128,2048]{2,1,0:T(8,128)(2,1)} %param.21) | copy-start | bytes 1572868
  627.0 24.0 %copy-start.25 = (f32[10,64]{1,0:T(8,128)S(1)}, f32[10,64]{1,0:T(8,128)}, u32[]{:S(2)}) copy-start(f32[10,64]{1,0:T(8,128)} %param.41) | copy-start | bytes 7684
  627.0 24.0 %copy-start.26 = (f32[10,64]{1,0:T(8,128)S(1)}, f32[10,64]{1,0:T(8,128)}, u32[]{:S(2)}) copy-start(f32[10,64]{1,0:T(8,128)} %param.40) | copy-start | bytes 7684
  627.0 25.3 %copy-start.28 = (f32[2,64]{1,0:T(2,128)S(1)}, f32[2,64]{1,0:T(2,128)}, u32[]{:S(2)}) copy-start(f32[2,64]{1,0:T(2,128)} %param.38) | copy-start | bytes 1540
  627.1 25.3 %copy-start.29 = (f32[2,64]{1,0:T(2,128)S(1)}, f32[2,64]{1,0:T(2,128)}, u32[]{:S(2)}) copy-start(f32[2,64]{1,0:T(2,128)} %param.37) | copy-start | bytes 1540
  635.1 20.2 %copy-start.4 = (f32[64,8192]{1,0:T(8,128)S(1)}, f32[64,8192]{1,0:T(8,128)}, u32[]{:S(2)}) copy-start(f32[64,8192]{1,0:T(8,128)} %param.30) | copy-start | bytes 6291460
  635.1 20.2 %copy-start.10 = (f32[64,8192]{1,0:T(8,128)S(1)}, f32[64,8192]{1,0:T(8,128)}, u32[]{:S(2)}) copy-start(f32[64,8192]{1,0:T(8,128)} %param.32) | copy-start | bytes 6291460
  635.1 20.2 %copy-start.11 = (f32[64,8192]{1,0:T(8,128)S(1)}, f32[64,8192]{1,0:T(8,128)}, u32[]{:S(2)}) copy-start(f32[64,8192]{1,0:T(8,128)} %param.31) | copy-start | bytes 6291460
  661.2 1.4 copy-start.7
  661.2 1.9 copy-start.14
  661.3 2.3 copy-start.15
  663.6 2.7 copy-start.13
  663.6 2.7 copy-start.18
  663.6 2.7 copy-start.19
  663.6 2.8 copy-start.20
  663.6 4.1 copy-start.22
  666.3 3.6 copy-start.6

commit v2 on v1

--- a/solution.py
+++ b/solution.py
@@ -1,4 +1,5 @@
 import functools
+import heapq
 import math
 
 import jax
@@ -112,11 +113,13 @@
     return [(None, {axis: (me + o) % size}) for o in range(1, size)]
 
 
-def gather(net, ro, src, place):
+def gather(net, ro, src, place, at_us=0.0, hop=11.0, over=1.0, hold=False):
     n, p, q = ro.length, ro.p, ro.q
     right, left = net.take(n - 1), net.take(n - 1)
     over_r, over_l, over_own = net.take(n - 1), net.take(n - 1), net.take(1)
     other = ro.dev(p, 1 - q)
+    if hold:
+        yield at_us
     at = lambda k: place(ro.index(k, q))
     across = lambda k: place(ro.index(k, 1 - q))
     ref = lambda j, k: src if j == 0 else at(k)
@@ -128,8 +131,8 @@
     pl.when(p + 1 < n)(lambda: go_right(0).start())
     pl.when(p > 0)(lambda: go_left(0).start())
     own.start()
-    yield
     for j in range(1, n):
+        yield at_us + hop * j
 
         @pl.when(p - j >= 0)
         def _():
@@ -145,7 +148,7 @@
                 pl.when(p > 0)(lambda: go_left(j).start())
             pass_l(j).start()
 
-        yield
+    yield at_us + hop * (n - 1) + over
     net.copy(over_own, src, across(p), other).wait_recv()
     for j in range(1, n):
 
@@ -179,16 +182,24 @@
         dst[at, :] = total.astype(dst.dtype)
         return 0
 
-    lax.fori_loop(0, dst.shape[0] // step, one, 0)
-
-
-def scatter_scratch(ro_length, rows, cols):
-    return [pltpu.VMEM((ro_length, rows, cols), BF16)] + [
-        pltpu.VMEM((ro_length - 1, rows, cols), BF16)
+    if len(dst.shape) == 3:
+
+        def layer(k, _):
+            add_rows(dst.at[k], [s.at[k] for s in srcs], step)
+            return 0
+
+        lax.fori_loop(0, dst.shape[0], layer, 0)
+    else:
+        lax.fori_loop(0, dst.shape[0] // step, one, 0)
+
+
+def scatter_scratch(ro_length, *shape):
+    return [pltpu.VMEM((ro_length, *shape), BF16)] + [
+        pltpu.VMEM((ro_length - 1, *shape), BF16)
     ] * 4
 
 
-def scatter(net, ro, part, result, room):
+def scatter(net, ro, part, result, room, at_us=0.0, first=2.0, hop=11.0, hold=False):
     sib, out_r, in_r, out_l, in_l = room
     n, p, q = ro.length, ro.p, ro.q
     right, left, pair = net.take(n - 1), net.take(n - 1), net.take(n)
@@ -200,10 +211,16 @@
     swap = lambda d: net.copy(pair + d, part(ro.index(d, 1 - q)), sib.at[d], other)
     send_r = lambda j: net.copy(right + j, out_r.at[j], in_r.at[j], ro.dev(p + 1, q))
     send_l = lambda j: net.copy(left + j, out_l.at[j], in_l.at[j], ro.dev(p - 1, q))
-    for d in order:
-        swap(d).start()
-    yield
+    if hold:
+        yield at_us
+    if n == 2:
+        swap(1 - p).start()
+        swap(p).start()
+    else:
+        for d in order:
+            swap(d).start()
     for j in range(n - 1):
+        yield at_us + first + hop * j
         dr, dl = n - 1 - j, j
 
         @pl.when(p < dr)
@@ -218,6 +235,8 @@
             @pl.when(p == 0)
             def _():
                 add_rows(out_r.at[j], [mine(dr), sib.at[dr]])
+                if j > 0:
+                    send_r(j - 1).wait_send()
 
             send_r(j).start()
 
@@ -233,10 +252,12 @@
             @pl.when(p == n - 1)
             def _():
                 add_rows(out_l.at[j], [mine(dl), sib.at[dl]])
+                if j > 0:
+                    send_l(j - 1).wait_send()
 
             send_l(j).start()
 
-        yield
+    yield at_us + first + hop * (n - 1)
     from_r, from_l = n - 1 - p, p
     swap(p).wait_recv()
 
@@ -266,22 +287,25 @@
         for d in order:
             swap(d).wait_send()
         for j in range(n - 1):
-            pl.when(p < n - 1 - j)(lambda: send_r(j).wait_send())
-            pl.when(p > j)(lambda: send_l(j).wait_send())
+            last = j == n - 2
+            pl.when((p < n - 1 - j) & ((p > 0) | last))(lambda: send_r(j).wait_send())
+            pl.when((p > j) & ((p < n - 1) | last))(lambda: send_l(j).wait_send())
 
     net.later.append(finish)
 
 
-def exchange(net, axis, src, place):
+def exchange(net, axis, src, place, at_us=0.0, last=15.0, hold=False):
     me, n = lax.axis_index(axis), lax.axis_size(axis)
     slots = net.take(n - 1)
+    if hold:
+        yield at_us
     near = net.local(src(me), place(me))
     sent = []
     for o in range(1, n):
         to = (me + o) % n
         sent.append(net.copy(slots + o - 1, src(to), place(me), {axis: to}))
         sent[-1].start()
-    yield
+    yield at_us + last
     near.wait()
     for o in range(1, n):
         at = (me + n - o) % n
@@ -289,28 +313,30 @@
     net.later.append(lambda: [s.wait_send() for s in sent])
 
 
-def together(*gens):
-    live = list(gens)
-    while live:
-        for g in list(live):
-            try:
-                next(g)
-            except StopIteration:
-                live.remove(g)
-        if live:
-            yield
-
-
-def then(first, makers):
-    yield from first
-    yield from together(*[m() for m in makers])
-
-
 def run(net, *gens):
-    for _ in together(*gens):
-        pass
+    waiting = []
+    for order, g in enumerate(gens):
+        heapq.heappush(waiting, (0.0, order, g))
+    while waiting:
+        now, order, g = heapq.heappop(waiting)
+        step = next(g, None)
+        if step is not None:
+            heapq.heappush(waiting, (max(step, now), order, g))
     for act in net.later:
         act()
+
+
+def merge(gens):
+    steps = [next(g, None) for g in gens]
+    while any(s is not None for s in steps):
+        at, k = min((s, i) for i, s in enumerate(steps) if s is not None)
+        yield at
+        steps[k] = next(gens[k], None)
+
+
+def follow(first, makers):
+    yield from merge(first)
+    yield from merge([m() for m in makers])
 
 
 VM = pl.BlockSpec(memory_space=pltpu.VMEM)
@@ -326,7 +352,7 @@
         scratch_shapes=[
             pltpu.SemaphoreType.DMA((slots,)),
             pltpu.SemaphoreType.DMA((slots,)),
-            pltpu.SemaphoreType.DMA((8,)),
+            pltpu.SemaphoreType.DMA((40,)),
         ]
         + room,
         compiler_params=pltpu.CompilerParams(
@@ -519,7 +545,9 @@
     small = jnp.concatenate([norm_gains, biases], axis=0).astype(BF16).astype(F32)
     small = jnp.pad(small, ((0, 4), (0, 128 - R)))
 
-    def first_kernel(tok, mix, out, vec, tok_f, mix_f, out_f, vec_f, send, recv, near):
+    def first_kernel(
+        tok, mix, out, vec, up, tok_f, mix_f, out_f, vec_f, up_r, send, recv, near
+    ):
         net = Net(send, recv, near)
         seq, sides = line_of("seq"), both_of("fsdp")
         s, f = lax.axis_index("seq"), lax.axis_index("fsdp")
@@ -532,42 +560,46 @@
 
         def mix_half(k):
             at = pl.ds(k * (S // 2), S // 2)
-            return lambda: gather(net, sides[k], mix_f.at[at, f], lambda i: mix_f.at[at, i])
+            return lambda: gather(
+                net, sides[k], mix_f.at[at, f], lambda i: mix_f.at[at, i], 20, 13, 13
+            )
 
         def out_half(k):
             at = pl.ds(k * (D // 2), D // 2)
-            return gather(net, sides[k], out.at[:, at], lambda i: out_f.at[i, :, at])
+            return gather(net, sides[k], out.at[:, at], lambda i: out_f.at[i, :, at], 0, 5, 5)
 
         def vec_next():
             vec_own.wait()
-            return gather(net, sides[0], vec_f.at[:, f], lambda i: vec_f.at[:, i])
+            return gather(net, sides[0], vec_f.at[:, f], lambda i: vec_f.at[:, i], 6, 1, 1)
 
         run(
             net,
-            then(
-                exchange(net, "seq", lambda i: mix.at[i], lambda i: mix_f.at[i, f]),
+            follow(
+                [exchange(net, "seq", lambda i: mix.at[i], lambda i: mix_f.at[i, f], 0, 20)],
                 [mix_half(0), mix_half(1)],
             ),
-            then(gather(net, seq, vec, lambda i: vec_f.at[i, f]), [vec_next]),
+            follow([gather(net, seq, vec, lambda i: vec_f.at[i, f], 0, 2, 1)], [vec_next]),
             out_half(0),
             out_half(1),
-            gather(net, seq, tok, lambda i: tok_f.at[i]),
+            gather(net, seq, tok, lambda i: tok_f.at[i], 0, 15),
+            exchange(net, "seq", lambda i: up.at[i], lambda i: up_r.at[i], 22, 60, True),
         )
         for o in owned:
             o.wait()
 
-    tok_full, mix_full, out_full, vec_full = call(
+    tok_full, mix_full, out_full, vec_full, up_mid = call(
         first_kernel,
         1,
-        (tokens[0], mix_low, out_low, small),
-        [HB] * 4,
+        (tokens[0], mix_low, out_low, small, up_low),
+        [HB] * 5,
         [
             ((S, T, D), BF16),
             ((S, F, R, 3 * W), BF16),
             ((F, R, D), BF16),
             ((S, F, 16, 128), F32),
+            ((S, R, U), BF16),
         ],
-        [HB] * 4,
+        [HB] * 5,
         [],
     )
     vectors = vec_full[:, :, :12, :R].transpose(2, 0, 1, 3).reshape(12, D)
@@ -586,34 +618,43 @@
     attended, log_sums = attend(mixed, start, slopes)
     out_part = jnp.dot(attended, out_own, preferred_element_type=F32).astype(BF16)
 
-    def second_kernel(part, cot, up, down, total, cot_f, up_r, down_f, send, recv, near, *room):
+    def second_kernel(part, cot, up, down, total, cot_f, up_f, down_f, send, recv, near, *room):
         net = Net(send, recv, near)
         seq, sides = line_of("seq"), both_of("fsdp")
         s, f = lax.axis_index("seq"), lax.axis_index("fsdp")
-        greet(everyone("seq") + everyone("fsdp"))
-        owned = [net.local(cot, cot_f.at[s]), net.local(down, down_f.at[f])]
+        greet(seq.partners() + everyone("fsdp"))
+        owned = [
+            net.local(cot, cot_f.at[s]),
+            net.local(down, down_f.at[f]),
+            net.local(up, up_f.at[:, f]),
+        ]
+
+        def up_half(k):
+            at = pl.ds(k * (S // 2), S // 2)
+            return gather(net, sides[k], up.at[at], lambda i: up_f.at[at, i], 0, 30, 34)
 
         def down_half(k):
             at = pl.ds(k * (RD // 2), RD // 2)
-            return gather(net, sides[k], down.at[at], lambda i: down_f.at[i, at])
+            return gather(net, sides[k], down.at[at], lambda i: down_f.at[i, at], 0, 29, 34)
 
         run(
             net,
-            scatter(net, seq, lambda i: part.at[i], total, room),
+            scatter(net, seq, lambda i: part.at[i], total, room, 0, 3, 13),
             down_half(0),
             down_half(1),
-            gather(net, seq, cot, lambda i: cot_f.at[i]),
-            exchange(net, "seq", lambda i: up.at[i], lambda i: up_r.at[i]),
+            gather(net, seq, cot, lambda i: cot_f.at[i], 0, 14),
+            up_half(0),
+            up_half(1),
         )
         for o in owned:
             o.wait()
 
-    attn_sum, cot_full, up_mid, down_full = call(
+    attn_sum, cot_full, up_full, down_full = call(
         second_kernel,
         2,
-        (out_part.reshape(S, T, D), cotangent[0], up_low, down_low),
+        (out_part.reshape(S, T, D), cotangent[0], up_mid, down_low),
         [VM, HB, HB, HB],
-        [((T, D), F32), ((S, T, D), BF16), ((S, R, U), BF16), ((F, RD, D), BF16)],
+        [((T, D), F32), ((S, T, D), BF16), ((S, F, R, U), BF16), ((F, RD, D), BF16)],
         [VM, HB, HB, HB],
         scatter_scratch(S // 2, T, D),
     )
@@ -621,69 +662,279 @@
     hidden_in = row_values + attn_sum + bias_values[3]
     normed_two = layer_norm(hidden_in, gain_values[1], bias_values[4]).astype(BF16)
 
-    def third_kernel(rows, up, rows_f, up_f, send, recv, near):
+    B = 2 * T
+    UT = min(256, U)
+    G = D // S
+    n = S // 2
+    down_items, items = U // UT, U // UT + S
+    per_step = -(-items // (n - 1))
+
+    def middle_kernel(
+        rows,
+        up,
+        down,
+        cot,
+        bias,
+        total,
+        result_out,
+        up_out,
+        down_out,
+        sums,
+        send,
+        recv,
+        near,
+        two,
+        up_v,
+        down_v,
+        cot_v,
+        act,
+        pre,
+        turn,
+        part_n,
+        part_r,
+        sib,
+        in_r,
+        in_l,
+    ):
         net = Net(send, recv, near)
-        seq, sides = line_of("seq"), both_of("fsdp")
-        s, f = lax.axis_index("seq"), lax.axis_index("fsdp")
-        greet(seq.partners() + everyone("fsdp"))
-        owned = [net.local(rows, rows_f.at[s]), net.local(up, up_f.at[:, f])]
-
-        def up_half(k):
-            at = pl.ds(k * (S // 2), S // 2)
-            return gather(net, sides[k], up.at[at], lambda i: up_f.at[at, i])
-
-        run(
-            net,
-            up_half(0),
-            up_half(1),
-            gather(net, seq, rows, lambda i: rows_f.at[i]),
+        ro = line_of("seq")
+        p, q = ro.p, ro.q
+        other = ro.dev(p, 1 - q)
+        loads = [net.local(up, up_v), net.local(down, down_v), net.local(cot, cot_v)]
+        sums[...] = jnp.zeros_like(sums)
+        greet(ro.partners())
+        block = lambda ref, i: ref.at[pl.ds(pl.multiple_of(i * T, T), T)]
+        place = lambda k, side: block(two, ro.index(k, side))
+        loads.append(net.local(rows, place(p, q)))
+        ag_r, ag_l, over = net.take(n - 1), net.take(n - 1), net.take(n)
+        rs_r, rs_l, pair = net.take(n - 1), net.take(n - 1), net.take(n)
+        ag_right = lambda k, src: net.copy(ag_r + p - k, src, place(k, q), ro.dev(p + 1, q))
+        ag_left = lambda k, src: net.copy(ag_l + k - p, src, place(k, q), ro.dev(p - 1, q))
+        ag_over = lambda k, src: net.copy(over + k, src, place(k, q), other)
+        mine = lambda d: block(part_n, ro.index(d, q))
+        swap = lambda d: net.copy(pair + d, block(part_n, ro.index(d, 1 - q)), sib.at[d], other)
+        move_r = lambda d: net.copy(rs_r + d - 1, in_r.at[d - 1], in_r.at[d - 1], ro.dev(p + 1, q))
+        move_l = lambda d: net.copy(rs_l + d, in_l.at[d], in_l.at[d], ro.dev(p - 1, q))
+        leave = lambda k: pltpu.make_async_copy(
+            part_r.at[pl.ds(pl.multiple_of(k * B, B), B)],
+            result_out.at[pl.ds(pl.multiple_of(k * B, B), B)],
+            near.at[8 + k],
         )
-        for o in owned:
-            o.wait()
-
-    two_full, up_full = call(
-        third_kernel,
+
+        pl.when(p + 1 < n)(lambda: ag_right(p, rows).start())
+        pl.when(p > 0)(lambda: ag_left(p, rows).start())
+        ag_over(p, rows).start()
+        for made in loads:
+            made.wait()
+
+        def arrive(e):
+            @pl.when((e > 0) & (p - e >= 0))
+            def _():
+                k = p - e
+                net.copy(ag_r + e - 1, place(k, q), place(k, q), other).wait_recv()
+                pl.when(p + 1 < n)(lambda: ag_right(k, place(k, q)).start())
+                ag_over(k, place(k, q)).start()
+
+            @pl.when((e > 0) & (p + e < n))
+            def _():
+                k = p + e
+                net.copy(ag_l + e - 1, place(k, q), place(k, q), other).wait_recv()
+                pl.when(p > 0)(lambda: ag_left(k, place(k, q)).start())
+                ag_over(k, place(k, q)).start()
+
+        def send_on(ends, e):
+            d = e - p
+
+            @pl.when(((p == 0) if ends else (p > 0)) & (d > p) & (d < n))
+            def _():
+                swap(d).wait_recv()
+                slot = in_r.at[d - 1]
+                if ends:
+                    add_rows(slot, [mine(d), sib.at[d]])
+                else:
+                    move_r(d).wait_recv()
+                    add_rows(slot, [slot, mine(d), sib.at[d]])
+                move_r(d).start()
+
+            d2 = n - 1 - (e - (n - 1 - p))
+
+            @pl.when(((p == n - 1) if ends else (p < n - 1)) & (d2 < p) & (d2 >= 0))
+            def _():
+                swap(d2).wait_recv()
+                slot = in_l.at[d2]
+                if ends:
+                    add_rows(slot, [mine(d2), sib.at[d2]])
+                else:
+                    move_l(d2).wait_recv()
+                    add_rows(slot, [slot, mine(d2), sib.at[d2]])
+                move_l(d2).start()
+
+        def feed_forward(k):
+            net.copy(over + k, place(k, 1 - q), place(k, 1 - q), other).wait_recv()
+            here = pl.ds(pl.multiple_of(k * B, B), B)
+
+            def hidden(i, _):
+                at = pl.ds(pl.multiple_of(i * UT, UT), UT)
+                value = jnp.dot(two[here, :], up_v[:, at], preferred_element_type=F32) + bias[:, at]
+                chance = 0.5 + 0.5 * lax.erf(value * 0.5**0.5)
+                slope = chance + value * (jnp.exp(value * value * -0.5) * (2 * math.pi) ** -0.5)
+                act[here, at] = (value * chance).astype(BF16)
+                grad = lax.dot_general(
+                    cot_v[here, :], down_v[at, :], (((1,), (1,)), ((), ())), preferred_element_type=F32
+                )
+                low = (grad * slope).astype(BF16)
+                pre[here, at] = low
+                sums[:, at] += jnp.sum(low.astype(F32), axis=0, keepdims=True)
+                return 0
+
+            lax.fori_loop(0, U // UT, hidden, 0)
+
+            def back(i, _):
+                at = pl.ds(pl.multiple_of(i * 512, 512), 512)
+                part_n[here, at] = lax.dot_general(
+                    pre[here, :], up_v[at, :], (((1,), (1,)), ((), ())), preferred_element_type=F32
+                ).astype(BF16)
+                return 0
+
+            lax.fori_loop(0, D // 512, back, 0)
+            swap(k).start()
+
+            def forth(i, _):
+                at = pl.ds(pl.multiple_of(i * 512, 512), 512)
+                part_r[here, at] = jnp.dot(
+                    act[here, :], down_v[:, at], preferred_element_type=F32
+                ).astype(BF16)
+                return 0
+
+            lax.fori_loop(0, D // 512, forth, 0)
+            leave(k).start()
+
+        def outward(e, _):
+            arrive(e)
+            send_on(False, e)
+            for side in (-1, 1):
+                k = p + side * e
+                pl.when((k >= 0) & (k < n) & ((e > 0) | (side > 0)))(lambda: feed_forward(k))
+            send_on(True, e)
+            return 0
+
+        lax.fori_loop(0, n, outward, 0)
+        up_leave = lambda i: pltpu.make_async_copy(
+            up_v.at[pl.ds(pl.multiple_of(i * G, G), G)],
+            up_out.at[pl.ds(pl.multiple_of(i * G, G), G)],
+            near.at[16 + i],
+        )
+        down_leave = lambda i: pltpu.make_async_copy(
+            down_v.at[pl.ds(pl.multiple_of(i * UT, UT), UT)],
+            down_out.at[pl.ds(pl.multiple_of(i * UT, UT), UT)],
+            near.at[4 + i],
+        )
+
+        def item(i, _):
+            @pl.when(i < down_items)
+            def _():
+                here = pl.ds(pl.multiple_of(i * UT, UT), UT)
+                turn[:UT, :] = act[:, here].T
+
+                def one(j, _):
+                    at = pl.ds(pl.multiple_of(j * 512, 512), 512)
+                    down_v[here, at] = jnp.dot(
+                        turn[:UT, :], cot_v[:, at], preferred_element_type=F32
+                    ).astype(BF16)
+                    return 0
+
+                lax.fori_loop(0, D // 512, one, 0)
+                down_leave(i).start()
+
+            @pl.when((i >= down_items) & (i < items))
+            def _():
+                c = i - down_items
+                here = pl.ds(pl.multiple_of(c * G, G), G)
+                turn[:G, :] = two[:, here].T
+
+                def one(j, _):
+                    at = pl.ds(pl.multiple_of(j * UT, UT), UT)
+                    up_v[here, at] = jnp.dot(
+                        turn[:G, :], pre[:, at], preferred_element_type=F32
+                    ).astype(BF16)
+                    return 0
+
+                lax.fori_loop(0, U // UT, one, 0)
+                up_leave(c).start()
+
+            return 0
+
+        def inward(e, _):
+            send_on(False, e)
+            lax.fori_loop((e - n) * per_step, (e - n + 1) * per_step, item, 0)
+            return 0
+
+        lax.fori_loop(n, 2 * n - 1, inward, 0)
+        swap(p).wait_recv()
+
+        @pl.when(p > 0)
+        def _():
+            move_r(p).wait_recv()
+
+        @pl.when(p < n - 1)
+        def _():
+            move_l(p).wait_recv()
+
+        @pl.when(p == 0)
+        def _():
+            add_rows(total, [mine(p), sib.at[p], in_l.at[p]])
+
+        @pl.when(p == n - 1)
+        def _():
+            add_rows(total, [mine(p), sib.at[p], in_r.at[p - 1]])
+
+        @pl.when((p > 0) & (p < n - 1))
+        def _():
+            add_rows(total, [mine(p), sib.at[p], in_r.at[p - 1], in_l.at[p]])
+
+        def last(k, _):
+            ag_over(k, place(k, q)).wait_send()
+            swap(k).wait_send()
+            leave(k).wait()
+            pl.when((k <= p) & (p + 1 < n))(lambda: ag_right(k, place(k, q)).wait_send())
+            pl.when((k >= p) & (p > 0))(lambda: ag_left(k, place(k, q)).wait_send())
+            pl.when(k > p)(lambda: move_r(k).wait_send())
+            pl.when(k < p)(lambda: move_l(k).wait_send())
+            return 0
+
+        lax.fori_loop(0, n, last, 0)
+        for i in range(down_items):
+            down_leave(i).wait()
+        for i in range(S):
+            up_leave(i).wait()
+
+    two_grad, result_part, up_part, down_part, pre_sum = call(
+        middle_kernel,
         3,
-        (normed_two, up_mid),
-        [HB, HB],
-        [((S, T, D), BF16), ((S, F, R, U), BF16)],
-        [HB, HB],
-        [],
-    )
-    two_full = two_full.reshape(L, D)
-    cot_full = cot_full.reshape(L, D)
-    up_own = up_full.reshape(D, U)
-    down_own = down_full.reshape(U, D)
-    pre_act = jnp.dot(two_full, up_own, preferred_element_type=F32) + mine(bias_values[6:10], U)
-    activated = gelu_exact(pre_act).astype(BF16)
-    result_part = jnp.dot(activated, down_own, preferred_element_type=F32).astype(BF16)
-    act_grad = jnp.einsum("td,fd->tf", cot_full, down_own, preferred_element_type=F32)
-    pre_grad = jax.vjp(gelu_exact, pre_act)[1](act_grad)[0].astype(BF16)
-    two_grad_part = jnp.einsum("tf,cf->tc", pre_grad, up_own, preferred_element_type=F32)
-    down_part = jnp.einsum("tf,td->fd", activated, cot_full, preferred_element_type=F32)
-    up_part = jnp.einsum("tc,tf->cf", two_full, pre_grad, preferred_element_type=F32)
-
-    def fourth_kernel(part, grad, total, share, send, recv, near, *room):
-        net = Net(send, recv, near)
-        seq, sides = line_of("seq"), both_of("fsdp")
-        greet(seq.partners() + everyone("fsdp"))
-
-        def half(k):
-            at = pl.ds(k * (D // 2), D // 2)
-            return scatter(
-                net, sides[k], lambda i: grad.at[i, :, at], share.at[:, at], room[5 + 5 * k : 10 + 5 * k]
-            )
-
-        run(net, scatter(net, seq, lambda i: part.at[i], total, room[:5]), half(0), half(1))
-
-    two_grad, down_share = call(
-        fourth_kernel,
-        4,
-        (two_grad_part.astype(BF16).reshape(S, T, D), down_part.astype(BF16).reshape(F, RD, D)),
-        [VM, VM],
-        [((T, D), F32), ((RD, D), F32)],
-        [VM, VM],
-        scatter_scratch(S // 2, T, D) + 2 * scatter_scratch(F // 2, RD, D // 2),
+        (
+            normed_two,
+            up_full.reshape(D, U),
+            down_full.reshape(U, D),
+            cot_full.reshape(L, D),
+            mine(bias_values[6:10], U)[None],
+        ),
+        [HB] * 4 + [VM],
+        [((T, D), F32), ((L, D), BF16), ((D, U), BF16), ((U, D), BF16), ((1, U), F32)],
+        [VM, HB, HB, HB, VM],
+        [
+            pltpu.VMEM((L, D), BF16),
+            pltpu.VMEM((D, U), BF16),
+            pltpu.VMEM((U, D), BF16),
+            pltpu.VMEM((L, D), BF16),
+            pltpu.VMEM((L, U), BF16),
+            pltpu.VMEM((L, U), BF16),
+            pltpu.VMEM((256, L), BF16),
+            pltpu.VMEM((L, D), BF16),
+            pltpu.VMEM((L, D), BF16),
+            pltpu.VMEM((n, T, D), BF16),
+            pltpu.VMEM((n - 1, T, D), BF16),
+            pltpu.VMEM((n - 1, T, D), BF16),
+        ],
     )
     upstream_float = cotangent[0].astype(F32)
     second_pull = jax.vjp(layer_norm, hidden_in, gain_values[1], bias_values[4])[1]
@@ -691,40 +942,60 @@
     hidden_gradient = upstream_float + hidden_part
     hidden_low = hidden_gradient.astype(BF16)
 
-    def fifth_kernel(rows, part, grad, rows_f, total, share, send, recv, near, *room):
+    def fifth_kernel(
+        rows, part, up, down, rows_f, total, up_s, down_s, send, recv, near, *room
+    ):
         net = Net(send, recv, near)
         seq, sides = line_of("seq"), both_of("fsdp")
         s = lax.axis_index("seq")
         greet(seq.partners() + everyone("fsdp"))
         own = net.local(rows, rows_f.at[s])
 
-        def half(k):
-            at = pl.ds(k * (U // 2), U // 2)
+        def up_half(k):
+            at = pl.ds(k * (S // 2), S // 2)
             return scatter(
-                net, sides[k], lambda i: grad.at[i, :, at], share.at[:, at], room[5 + 5 * k : 10 + 5 * k]
+                net, sides[k], lambda i: up.at[at, i], up_s.at[at], room[5 + 5 * k : 10 + 5 * k], 0, 22, 44
+            )
+
+        def down_half(k):
+            at = pl.ds(k * (D // 2), D // 2)
+            return scatter(
+                net,
+                sides[k],
+                lambda i: down.at[i, :, at],
+                down_s.at[:, at],
+                room[15 + 5 * k : 20 + 5 * k],
+                0,
+                22,
+                44,
             )
 
         run(
             net,
             gather(net, seq, rows, lambda i: rows_f.at[i]),
             scatter(net, seq, lambda i: part.at[i], total, room[:5]),
-            half(0),
-            half(1),
+            down_half(0),
+            down_half(1),
+            up_half(0),
+            up_half(1),
         )
         own.wait()
 
-    hidden_full, result_sum, up_mid_grad = call(
+    hidden_full, result_sum, up_mid_grad, down_share = call(
         fifth_kernel,
         5,
         (
             hidden_low,
             result_part.reshape(S, T, D),
-            up_part.astype(BF16).reshape(S, F, R, U).transpose(1, 0, 2, 3).reshape(F, S * R, U),
+            up_part.reshape(S, F, R, U),
+            down_part.reshape(F, RD, D),
         ),
-        [HB, VM, VM],
-        [((S, T, D), BF16), ((T, D), F32), ((S * R, U), BF16)],
-        [HB, VM, VM],
-        scatter_scratch(S // 2, T, D) + 2 * scatter_scratch(F // 2, S * R, U // 2),
+        [HB, VM, VM, VM],
+        [((S, T, D), BF16), ((T, D), F32), ((S, R, U), BF16), ((RD, D), F32)],
+        [HB, VM, VM, VM],
+        scatter_scratch(S // 2, T, D)
+        + 2 * scatter_scratch(F // 2, S // 2, R, U)
+        + 2 * scatter_scratch(F // 2, RD, D // 2),
     )
     output = (hidden_in + result_sum + bias_values[5]).astype(BF16)[None]
     hidden_full = hidden_full.reshape(L, D)
@@ -745,32 +1016,31 @@
         net = Net(send, recv, near)
         seq, sides = line_of("seq"), both_of("fsdp")
         greet(everyone("seq") + everyone("fsdp"))
-        C = S * R // 2
 
         def mix_half(k):
-            at = pl.ds(k * C, C)
+            at = pl.ds(k * (S // 2), S // 2)
             return scatter(
-                net, sides[k], lambda i: mix.at[i, at], mix_r.at[at], room[5 + 5 * k : 10 + 5 * k]
+                net, sides[k], lambda i: mix.at[at, i], mix_r.at[at], room[5 + 5 * k : 10 + 5 * k], 0, 11, 22
             )
 
         def out_half(k):
             at = pl.ds(k * (D // 2), D // 2)
             return scatter(
-                net, sides[k], lambda i: out.at[i, :, at], out_s.at[:, at], room[15 + 5 * k : 20 + 5 * k]
+                net, sides[k], lambda i: out.at[i, :, at], out_s.at[:, at], room[15 + 5 * k : 20 + 5 * k], 0, 11, 22
             )
 
         run(
             net,
-            then(
-                together(mix_half(0), mix_half(1)),
+            follow(
+                [mix_half(0), mix_half(1)],
                 [
                     lambda: exchange(
-                        net, "seq", lambda i: mix_r.at[pl.ds(i * R, R)], lambda i: mix_s.at[i]
+                        net, "seq", lambda i: mix_r.at[i], lambda i: mix_s.at[i], 34
                     )
                 ],
             ),
             scatter(net, seq, lambda i: part.at[i], total, room[:5]),
-            exchange(net, "seq", lambda i: up.at[i], lambda i: up_s.at[i]),
+            exchange(net, "seq", lambda i: up.at[i], lambda i: up_s.at[i], 0, 45),
             out_half(0),
             out_half(1),
         )
@@ -780,19 +1050,16 @@
         6,
         (
             one_grad_part.astype(BF16).reshape(S, T, D),
-            mix_grad.astype(BF16)
-            .reshape(S, F, R, 3 * W)
-            .transpose(1, 0, 2, 3)
-            .reshape(F, S * R, 3 * W),
+            mix_grad.astype(BF16).reshape(S, F, R, 3 * W),
             out_grad.astype(BF16).reshape(F, R, D),
-            up_mid_grad.reshape(S, R, U),
+            up_mid_grad,
         ),
         [VM, VM, VM, HB],
         [((T, D), F32), ((S, R, 3 * W), BF16), ((R, D), F32), ((S, R, U), BF16)],
         [VM, HB, VM, HB],
-        [pltpu.VMEM((S * R, 3 * W), BF16)]
+        [pltpu.VMEM((S, R, 3 * W), BF16)]
         + scatter_scratch(S // 2, T, D)
-        + 2 * scatter_scratch(F // 2, S * R // 2, 3 * W)
+        + 2 * scatter_scratch(F // 2, S // 2, R, 3 * W)
         + 2 * scatter_scratch(F // 2, R, D // 2),
     )
     first_pull = jax.vjp(layer_norm, row_values, gain_values[0], bias_values[0])[1]
@@ -815,7 +1082,7 @@
             jnp.sum(hidden_gradient, axis=0)[None],
             shift_two_gradient[None],
             jnp.sum(upstream_float, axis=0)[None],
-            spread(jnp.sum(pre_grad.astype(F32), axis=0), 4),
+            spread(pre_sum[0], 4),
         ],
         axis=0,
     )

time: 684 us -> 597 us (0.87)
  matrix products: 75.5 us -> 25.7 us
  Pallas kernels: 526 us -> 502 us
  other arithmetic: 51.4 us -> 41.8 us
    dot_general x6 -> x0, matrix products: 51.2 us -> none  [the longest x1 17.7 us: body(): jnp.einsum('td,fd->tf', cot_full, down_own, preferred_element_type=F32)]
    pallas_call x7 -> x6, Pallas kernels: 506 us -> 482 us  [comm_call(): pl.pallas_call(kernel, out_shape=[jax.ShapeDtypeStruct(*o) for o in outs]...]
where the time goes in v2:
time: 597 us; the launch traced here: 590 us
  Pallas kernels  502 us (84%)
  other arithmetic  41.8 us (7%)
  matrix products  25.7 us (4%)
  local copies, waits for them, and re-layouts  19.4 us (3%)
    pallas_call x6, Pallas kernels, comm_call(): pl.pallas_call(kernel, out_shape=[jax.ShapeDtypeStruct(*o) for o in outs]...  482 us
    add x6, other arithmetic, body(): new_average = avg_decay * average + (1.0 - avg_decay) * new_weight  14 us

profile of v2, /device:TPU:0, one launch (start us, length us, event | category | flops | bytes accessed | tf_op | source)
XLA Modules:
  0.0 590.1 jit_solution(3775104083119887946)
XLA Ops:
  0.7 1.5 convert_element_type.87
  2.3 0.4 copy.67
  2.7 1.7 reshape.277.mix
  4.6 1.1 copy.66
  5.6 0.7 convert_element_type.88.out
  6.4 0.6 fusion.21.vec
  7.0 90.1 %shard_map.356 = (bf16[8,128,2048]{2,1,0:T(8,128)(2,1)}, bf16[8,4,64,768]{3,2,1,0:T(8,128)(2,1)}, bf16[4,64,2048]{2,1,0:T(8,128)(2,1)}, f32[8,4,16,128]{3,2,1,0:T(8,128)}, bf16[8,64,1024]{2,1,0:T(8,128)(2,1)}) custom-call(bf16[128,2048]{1,0:T(8,128)(2,1)} %bitcast.98, bf16[8,64,768]{2,1,0:T(8,128)(2,1)} %reshape.277.mix, ...), custom_call_target="tpu_custom_call" | custom-call | tf_op jit(solution)/shard_map/pallas_call | solution.py:347
  97.0 3.0 convert_reduce_fusion
  100.0 0.5 copy-done
  100.5 1.2 multiply_reduce_fusion
  101.8 0.4 slice_reduce_fusion
  102.3 4.6 add_convert_fusion
  107.3 6.6 %add_convert_fusion.1.q_ref.k_ref.v_ref = bf16[1024,768]{1,0:T(8,128)(2,1)S(1)} fusion(bf16[1024,2048]{1,0:T(8,128)(2,1)} %bitcast.107, bf16[2048,768]{1,0:T(8,128)(2,1)} %bitcast.129, f32[768]{0:T(1024)S(1)} %pad_maximum_fusion), kind=kOutput, calls=%fused_computation.13 | convolution fusion | flops 3222798336 | bytes 8915968 | tf_op jit(solution)/shard_map/dot_general | solution.py:617
  113.9 0.5 convert_reduce_fusion.1
  114.4 10.3 %shard_map.357 = (bf16[1024,256]{1,0:T(8,128)(2,1)S(1)}, f32[2,2,1024]{2,1,0:T(2,128)S(1)}) custom-call(f32[4]{0:T(128)S(1)} %multiply_exponential_fusion.slopes_ref, s32[1,1024]{1,0:T(1,128)S(1)} %bitcast.95, bf16[1024,768]{1,0:T(8,128)(2,1)S(1)} %add_convert_fusion.1.q_ref.k_ref.v_ref, bf16[1024,768]{1,0:T(8,128)(2,1)S(1)} %add_convert_fusion.1.q_ref.k_ref.v_ref, ...), custom_call_target="tpu_custom_call" | custom-call | tf_op jit(solution)/shard_map/pallas_call | solution.py:462
  124.7 3.2 convolution_convert_fusion
  127.9 1.1 convert_element_type.95.down
  129.1 101.9 %shard_map.358 = (f32[128,2048]{1,0:T(8,128)}, bf16[8,128,2048]{2,1,0:T(8,128)(2,1)}, bf16[8,4,64,1024]{3,2,1,0:T(8,128)(2,1)}, bf16[4,256,2048]{2,1,0:T(8,128)(2,1)}) custom-call(bf16[8,128,2048]{2,1,0:T(8,128)(2,1)} %bitcast.97, bf16[128,2048]{1,0:T(8,128)(2,1)} %bitcast.103, bf16[8,64,1024]{2,1,0:T(8,128)(2,1)} %get-tuple-element.52.up, ...), custom_call_target="tpu_custom_call" | custom-call | tf_op jit(solution)/shard_map/pallas_call | solution.py:347
  231.0 1.6 fusion.31
  232.6 0.3 multiply_reduce_fusion.3
  233.1 1.0 add_convert_fusion.4.rows
  234.3 0.6 dynamic_slice.11
  234.8 91.4 %shard_map.359 = (f32[128,2048]{1,0:T(8,128)}, bf16[1024,2048]{1,0:T(8,128)(2,1)}, bf16[2048,1024]{1,0:T(8,128)(2,1)}, bf16[1024,2048]{1,0:T(8,128)(2,1)}, f32[1,1024]{1,0:T(1,128)}) custom-call(bf16[128,2048]{1,0:T(8,128)(2,1)} %add_convert_fusion.4.rows, bf16[2048,1024]{1,0:T(8,128)(2,1)} %bitcast.111, bf16[1024,2048]{1,0:T(8,128)(2,1)} %bitcast.112, ...), custom_call_target="tpu_custom_call" | custom-call | tf_op jit(solution)/shard_map/pallas_call | solution.py:347
  326.3 1.7 multiply_reduce_fusion.1
  328.0 0.4 fusion.30
  328.4 0.6 copy-done.9
  329.1 1.0 fusion.27.rows
  330.0 97.1 %shard_map.360 = (bf16[8,128,2048]{2,1,0:T(8,128)(2,1)}, f32[128,2048]{1,0:T(8,128)}, bf16[8,64,1024]{2,1,0:T(8,128)(2,1)}, f32[256,2048]{1,0:T(8,128)}) custom-call(bf16[128,2048]{1,0:T(8,128)(2,1)} %fusion.27.rows, bf16[8,128,2048]{2,1,0:T(8,128)(2,1)} %bitcast.104, bf16[8,4,64,1024]{3,2,1,0:T(8,128)(2,1)} %bitcast.105, bf16[4,256,2048]{2,1,0:T(8,128)(2,1)} %bitcast.106), custom_call_target="tpu_custom_call" | custom-call | tf_op jit(solution)/shard_map/pallas_call | solution.py:347
  427.2 4.6 convolution_convert_fusion.3
  431.8 1.3 convolution_convert_fusion.4.g_ref
  433.1 9.7 %shard_map.361 = (bf16[1024,256]{1,0:T(8,128)(2,1)S(1)}, bf16[1024,256]{1,0:T(8,128)(2,1)S(1)}, bf16[1024,256]{1,0:T(8,128)(2,1)S(1)}) custom-call(f32[4]{0:T(128)S(1)} %multiply_exponential_fusion.slopes_ref, s32[1,1024]{1,0:T(1,128)S(1)} %bitcast.96, bf16[1024,768]{1,0:T(8,128)(2,1)S(1)} %add_convert_fusion.1.q_ref.k_ref.v_ref, ...), custom_call_target="tpu_custom_call" | custom-call | tf_op jit(solution)/shard_map/pallas_call | solution.py:479
  443.0 1.9 fusion.3
  444.9 4.9 convolution_convert_fusion.2
  449.8 5.0 convolution_convert_fusion.1
  454.8 85.0 %shard_map.362 = (f32[128,2048]{1,0:T(8,128)}, bf16[8,64,768]{2,1,0:T(8,128)(2,1)}, f32[64,2048]{1,0:T(8,128)}, bf16[8,64,1024]{2,1,0:T(8,128)(2,1)}) custom-call(bf16[8,128,2048]{2,1,0:T(8,128)(2,1)} %bitcast.113, bf16[8,4,64,768]{3,2,1,0:T(8,128)(2,1)} %bitcast.117, bf16[4,64,2048]{2,1,0:T(8,128)(2,1)} %bitcast.118, bf16[8,64,1024]{2,1,0:T(8,128)(2,1)} %get-tuple-element.67.up), custom_call_target="tpu_custom_call" | custom-call | tf_op jit(solution)/shard_map/pallas_call | solution.py:347
  539.8 1.7 fusion.29
  541.6 0.5 fusion.11
  542.1 1.5 convert_reduce_fusion.4
  543.9 0.3 convert_reduce_fusion.2
  544.3 0.5 broadcast.263
  544.8 0.7 reduce.40
  545.6 0.7 reduce.41
  546.3 0.3 dynamic_update_slice.13
  547.2 0.7 pad.12.vec
  547.9 16.3 %shard_map.363 = f32[16,128]{1,0:T(8,128)} custom-call(f32[8,4,16,128]{3,2,1,0:T(8,128)} %pad.12.vec), custom_call_target="tpu_custom_call" | custom-call | tf_op jit(solution)/shard_map/pallas_call | solution.py:347
  564.2 1.3 add_multiply_fusion.4
  565.6 1.3 add_multiply_fusion.5
  567.1 0.2 copy.61
  567.3 1.1 copy-done.12
  568.4 0.7 copy-done.5
  569.1 0.6 copy-done.11
  569.7 3.3 add_multiply_fusion.1
  573.1 2.5 reshape.309
  575.6 0.9 copy.57
  576.5 0.5 copy.63
  577.0 1.0 copy-done.8
  578.0 0.5 copy-done.18
  578.6 2.9 add_multiply_fusion.2
  581.5 1.3 add_multiply_fusion.3
  582.8 0.9 copy-done.14
  583.7 0.6 copy-done.15
  584.3 0.7 copy-done.7
  585.0 3.9 add_multiply_fusion
  589.0 0.9 fusion.13
  (116 shorter events, 2.8 us)
Async XLA Ops:
  2.3 2.1 copy-start.4
  4.4 1.2 copy-start.16
  4.5 1.8 copy-start.28
  4.5 1.8 copy-start.33
  97.0 3.5 copy-start
  100.5 1.2 copy-start.27
  107.3 6.6 %copy-start.29 = (s32[1,1024]{1,0:T(1,128)S(1)}, s32[1,1024]{1,0:T(1,128)}, u32[]{:S(2)}) copy-start(s32[1,1024]{1,0:T(1,128)} %param.22) | copy-start | bytes 12292
  114.4 10.3 %copy-start.22 = (bf16[4,64,2048]{2,1,0:T(8,128)(2,1)S(1)}, bf16[4,64,2048]{2,1,0:T(8,128)(2,1)}, u32[]{:S(2)}) copy-start(bf16[4,64,2048]{2,1,0:T(8,128)(2,1)} %get-tuple-element.51) | copy-start | bytes 3145732
  124.7 3.3 copy-start.6
  326.3 1.7 copy-start.10
  328.0 1.0 copy-start.9
  427.2 4.6 copy-start.23
  427.2 4.6 copy-start.36
  433.1 9.9 %copy-start.1 = (bf16[8,128,2048]{2,1,0:T(8,128)(2,1)S(1)}, bf16[8,128,2048]{2,1,0:T(8,128)(2,1)}, u32[]{:S(2)}) copy-start(bf16[8,128,2048]{2,1,0:T(8,128)(2,1)} %get-tuple-element.47) | copy-start | bytes 12582916
  444.9 5.0 copy-start.37
  454.8 85.0 %copy-start.2 = (bf16[1,128,2048]{2,1,0:T(8,128)(2,1)S(1)}, bf16[1,128,2048]{2,1,0:T(8,128)(2,1)}, u32[]{:S(2)}) copy-start(bf16[1,128,2048]{2,1,0:T(8,128)(2,1)} %param.21) | copy-start | bytes 1572868
  539.8 1.7 copy-start.3
  542.1 4.2 copy-start.32
  543.6 20.6 %copy-start.30 = (f32[10,64]{1,0:T(8,128)S(1)}, f32[10,64]{1,0:T(8,128)}, u32[]{:S(2)}) copy-start(f32[10,64]{1,0:T(8,128)} %param.41) | copy-start | bytes 7684
  543.6 20.6 %copy-start.31 = (f32[10,64]{1,0:T(8,128)S(1)}, f32[10,64]{1,0:T(8,128)}, u32[]{:S(2)}) copy-start(f32[10,64]{1,0:T(8,128)} %param.40) | copy-start | bytes 7684
  543.6 21.9 %copy-start.34 = (f32[2,64]{1,0:T(2,128)S(1)}, f32[2,64]{1,0:T(2,128)}, u32[]{:S(2)}) copy-start(f32[2,64]{1,0:T(2,128)} %param.38) | copy-start | bytes 1540
  543.6 21.9 %copy-start.35 = (f32[2,64]{1,0:T(2,128)S(1)}, f32[2,64]{1,0:T(2,128)}, u32[]{:S(2)}) copy-start(f32[2,64]{1,0:T(2,128)} %param.37) | copy-start | bytes 1540
  544.2 22.6 %copy-start.20 = (bf16[8,64,1024]{2,1,0:T(8,128)(2,1)S(1)}, bf16[8,64,1024]{2,1,0:T(8,128)(2,1)}, u32[]{:S(2)}) copy-start(bf16[8,64,1024]{2,1,0:T(8,128)(2,1)} %get-tuple-element.71) | copy-start | bytes 3145732
  566.8 1.6 copy-start.12
  567.1 2.0 copy-start.5
  567.1 2.7 copy-start.11
  575.6 1.4 copy-start.19
  576.5 1.5 copy-start.8
  576.5 2.0 copy-start.18
  578.5 3.0 copy-start.17
  578.5 3.0 copy-start.24
  578.5 3.0 copy-start.25
  578.5 3.0 copy-start.26
  578.5 4.3 copy-start.13
  578.5 5.1 copy-start.14
  578.6 5.7 copy-start.15
  581.5 3.5 copy-start.7
  585.0 4.0 copy-start.21
